TPU v7x, 32 devices: a whole 2x2x4 slice. The times are simulated.
32 devices in a mesh: groups: 2 (over y), col: 4 (over z), row: 4 (over x, core).
Axes of the slice: x: 2, y: 2, z: 4, core: 2. Of those that a mesh axis runs over, the one named last changes fastest.
Arguments:
- p_blocks: float32 [8, 256, 4096], P(('groups', 'col'), 'row'), parts along dimension 0, may hold values from -0.72 to 0.72
- products: int32 [8, 4, 3, 2048], P(('groups', 'col'), 'row'), parts along dimension 0, may hold values from 0 to 255, as said below
Outputs:
- square_blocks: float32 [8, 32, 4096], P(('groups', 'row'), 'col'), parts along dimension 0
There are 2 independent parts, one for each index of `groups`. A program takes and returns all parts, laid end to end along the dimension named above; each array names one. Nothing has to cross between parts.
Inputs may be any that keep to these rules, and one draw needn't show every extreme that they name: `products`: in each list, first lies below 256, second below 64, target at most 32. Live entries (target below 32) stand before all padding entries, which are (255, 63, 32). Every list has at least one live entry; one grid cell of each part has all 2048 entries live.
All inputs are finite; a program needn't handle non-finite values.
Results may differ from a plain program's by a relative error of at most 0.0001.
Values sent between devices are 32-bit elements; how exact they have to be, the bound alone decides.
No kernel may reach another device: no remote copies, remote signals or barrier semaphores. Data moves between devices by JAX's collectives and lax.ppermute only.
A program may use at most 192 MiB of HBM per device.

v0:
```python
import jax
import jax.numpy as jnp
from jax import lax
from jax.sharding import PartitionSpec as P

BLK = 64
BB = 4096
SC = 8
TILE = 128
NBAT = 16


batches_per_turn = 4


def per_device(p_blocks, products):
    own_blocks = p_blocks[0]
    product_list = products[0, 0]
    grid_columns = lax.axis_size("col")
    row_panel = lax.all_gather(own_blocks, "row", axis=0, tiled=True)
    panel_count = row_panel.shape[0]
    turned_panel = jnp.swapaxes(row_panel.reshape(panel_count, BLK, BLK), 1, 2).reshape(
        panel_count, BB
    )
    start_sums = jnp.zeros((grid_columns * SC, BB), jnp.float32)
    span = batches_per_turn * TILE

    def advance(number, partial_sums):
        chosen = lax.dynamic_slice_in_dim(product_list, number * span, span, 1)
        left = jnp.take(turned_panel, chosen[0], axis=0).reshape(span, BLK, BLK)
        right = jnp.take(own_blocks, chosen[1], axis=0).reshape(span, BLK, BLK)
        result = jnp.einsum("nik,nkj->nij", left, right, precision=lax.Precision.HIGHEST)
        return partial_sums.at[chosen[2]].add(result.reshape(span, BB), mode="drop")

    partial_sums = lax.fori_loop(0, NBAT // batches_per_turn, advance, start_sums)
    owned = lax.psum_scatter(partial_sums, "col", scatter_dimension=0, tiled=True)
    return owned[None]


def solution(mesh):
    return jax.shard_map(
        per_device,
        mesh=mesh,
        in_specs=(P(("groups", "col"), "row", None), P(("groups", "col"), "row", None, None)),
        out_specs=P(("groups", "row"), "col", None),
        check_vma=False,
    )
```

profile of v0, /device:TPU:0, one launch (start us, length us, event | category | flops | bytes accessed | tf_op | source)
XLA Modules:
  0.0 673.1 jit_solution(11921097616459311067)
XLA Ops:
  6.5 3.3 copy.27
  9.8 0.0 all-gather.3.cloned.1.call-update
  9.8 0.0 reduce-scatter.2.cloned.1.call-start
  9.9 0.8 copy.33
  10.7 36.5 %all-gather.3.cloned.1.call-done = f32[1,256,4096]{2,0,1:T(1,128)} async-done(((f32[1,64,4096]{2,0,1:T(1,128)}), f32[1,256,4096]{2,0,1:T(1,128)}) %all-gather.3.cloned.1.call-update) | async-done | bytes 4194320 | tf_op jit(solution)/shard_map/all_gather | solution.py:20
  47.2 10.2 %copy.28 = f32[1,256,4096]{1,2,0:T(8,128)} copy(f32[1,256,4096]{2,0,1:T(1,128)} %all-gather.3.cloned.1.call-done) | data formatting | bytes 8388608 | tf_op jit(solution)/shard_map/all_gather | solution.py:20
  57.4 6.6 copy.29
  64.0 5.8 copy.30
  69.8 573.8 %while.13 = (s32[]{:T(128)}, f32[32,4096]{1,0:T(8,128)S(1)}, s32[3,2048]{1,0:T(4,128)S(1)}, f32[256,4096]{1,0:T(8,128)}, f32[64,4096]{1,0:T(8,128)S(1)}, /*index...) while((s32[]{:T(128)}, f32[32,4096]{1,0:T(8,128)S(1)}, s32[3,2048]{1,0:T(4,128)S(1)}, ...), condition=%wide.region_2.3_spmd, body=%wide.region_0.2_spmd.sunk | while | flops 1616916992 | bytes 218144976 | solution.py:35
  70.0 0.1 compare_select_fusion.6
  70.2 5.1 gather_fusion.1
  75.2 9.0 %copy.42 = f32[512,4096]{0,1:T(8,128)} copy(f32[512,4096]{1,0:T(8,128)} %gather_fusion.1) | data formatting | bytes 16777216 | tf_op jit(solution)/shard_map/while/body/eval_jaxpr/jit(_take)/gather | solution.py:31
  84.3 8.5 %broadcast_select_fusion.5 = f32[512,64,64]{0,2,1:T(8,128)} fusion(f32[512,64,64]{0,2,1:T(8,128)} %bitcast.51, pred[512]{0:T(512)(128)(4,1)S(1)} %compare_and_fusion.5), kind=kLoop, calls=%fused_computation.3.clone.1 | loop fusion | flops 2097152 | bytes 16777728 | tf_op jit(solution)/shard_map/while/body/eval_jaxpr/jit(_take)/select_n | solution.py:31
  92.8 11.0 %gather_fusion = f32[512,4096]{1,0:T(8,128)} fusion(f32[256,4096]{1,0:T(8,128)} %get-tuple-element.198, s32[1024]{0:T(1024)S(1)} %pad_clamp_fusion.4), kind=kCustom, calls=%fused_computation.clone.1 | custom fusion | bytes 16779264 | tf_op jit(solution)/shard_map/while/body/eval_jaxpr/jit(_take)/gather | solution.py:30
  103.8 9.0 %copy.40 = f32[512,4096]{0,1:T(8,128)} copy(f32[512,4096]{1,0:T(8,128)} %gather_fusion) | data formatting | bytes 16777216 | tf_op jit(solution)/shard_map/while/body/eval_jaxpr/jit(_take)/gather | solution.py:30
  112.8 8.5 %broadcast_select_fusion.4 = f32[512,64,64]{0,2,1:T(8,128)} fusion(f32[512,64,64]{0,2,1:T(8,128)} %bitcast.52, pred[512]{0:T(512)(128)(4,1)S(1)} %compare_and_fusion.4), kind=kLoop, calls=%fused_computation.4.clone.1 | loop fusion | flops 2097152 | bytes 16777728 | tf_op jit(solution)/shard_map/while/body/eval_jaxpr/jit(_take)/select_n | solution.py:30
  121.3 16.3 %copy.41 = f32[512,64,64]{2,1,0:T(8,128)} copy(f32[512,64,64]{0,2,1:T(8,128)} %broadcast_select_fusion.4) | data formatting | bytes 16777216 | tf_op jit(solution)/shard_map/while/body/eval_jaxpr/jit(_take)/select_n | solution.py:30
  137.6 16.2 %copy.43 = f32[512,64,64]{2,1,0:T(8,128)} copy(f32[512,64,64]{0,2,1:T(8,128)} %broadcast_select_fusion.5) | data formatting | bytes 16777216 | tf_op jit(solution)/shard_map/while/body/eval_jaxpr/jit(_take)/select_n | solution.py:31
  153.8 23.7 %fusion.8 = f32[512,64,64]{2,1,0:T(8,128)} fusion(f32[512,64,64]{2,1,0:T(8,128)} %copy.41, f32[512,64,64]{2,1,0:T(8,128)} %copy.43), kind=kOutput, calls=%fused_computation.17.clone.1 | convolution fusion | flops 1610612736 | bytes 25165824 | tf_op jit(solution)/shard_map/while/body/eval_jaxpr/nik,nkj->nij/dot_general | solution.py:32
  177.5 12.7 %copy.44 = f32[512,64,64]{0,2,1:T(8,128)} copy(f32[512,64,64]{2,1,0:T(8,128)} %fusion.8) | data formatting | bytes 16777216 | tf_op jit(solution)/shard_map/while/body/eval_jaxpr/nik,nkj->nij/dot_general | solution.py:32
  190.3 8.9 %copy.45 = f32[512,4096]{1,0:T(8,128)} copy(f32[512,4096]{0,1:T(8,128)} %bitcast.50) | data formatting | bytes 16777216 | tf_op jit(solution)/shard_map/while/body/eval_jaxpr/reshape | solution.py:33
  199.2 14.2 %scatter_fusion = f32[32,4096]{1,0:T(8,128)S(1)} fusion(f32[32,4096]{1,0:T(8,128)S(1)} %get-tuple-element.185, s32[512]{0:T(512)S(1)} %bitcast.55, f32[512,4096]{1,0:T(8,128)} %copy.45), kind=kCustom, calls=%fused_computation.2.clone.1 | custom fusion | flops 2097152 | bytes 25167872 | tf_op jit(solution)/shard_map/while/body/eval_jaxpr/scatter-add | solution.py:33
  213.4 0.1 compare_select_fusion.6
  213.6 5.1 gather_fusion.1
  218.6 9.0 %copy.42 = f32[512,4096]{0,1:T(8,128)} copy(f32[512,4096]{1,0:T(8,128)} %gather_fusion.1) | data formatting | bytes 16777216 | tf_op jit(solution)/shard_map/while/body/eval_jaxpr/jit(_take)/gather | solution.py:31
  227.7 8.5 %broadcast_select_fusion.5 = f32[512,64,64]{0,2,1:T(8,128)} fusion(f32[512,64,64]{0,2,1:T(8,128)} %bitcast.51, pred[512]{0:T(512)(128)(4,1)S(1)} %compare_and_fusion.5), kind=kLoop, calls=%fused_computation.3.clone.1 | loop fusion | flops 2097152 | bytes 16777728 | tf_op jit(solution)/shard_map/while/body/eval_jaxpr/jit(_take)/select_n | solution.py:31
  236.2 11.0 %gather_fusion = f32[512,4096]{1,0:T(8,128)} fusion(f32[256,4096]{1,0:T(8,128)} %get-tuple-element.198, s32[1024]{0:T(1024)S(1)} %pad_clamp_fusion.4), kind=kCustom, calls=%fused_computation.clone.1 | custom fusion | bytes 16779264 | tf_op jit(solution)/shard_map/while/body/eval_jaxpr/jit(_take)/gather | solution.py:30
  247.2 9.0 %copy.40 = f32[512,4096]{0,1:T(8,128)} copy(f32[512,4096]{1,0:T(8,128)} %gather_fusion) | data formatting | bytes 16777216 | tf_op jit(solution)/shard_map/while/body/eval_jaxpr/jit(_take)/gather | solution.py:30
  256.2 8.5 %broadcast_select_fusion.4 = f32[512,64,64]{0,2,1:T(8,128)} fusion(f32[512,64,64]{0,2,1:T(8,128)} %bitcast.52, pred[512]{0:T(512)(128)(4,1)S(1)} %compare_and_fusion.4), kind=kLoop, calls=%fused_computation.4.clone.1 | loop fusion | flops 2097152 | bytes 16777728 | tf_op jit(solution)/shard_map/while/body/eval_jaxpr/jit(_take)/select_n | solution.py:30
  264.7 16.3 %copy.41 = f32[512,64,64]{2,1,0:T(8,128)} copy(f32[512,64,64]{0,2,1:T(8,128)} %broadcast_select_fusion.4) | data formatting | bytes 16777216 | tf_op jit(solution)/shard_map/while/body/eval_jaxpr/jit(_take)/select_n | solution.py:30
  281.0 16.2 %copy.43 = f32[512,64,64]{2,1,0:T(8,128)} copy(f32[512,64,64]{0,2,1:T(8,128)} %broadcast_select_fusion.5) | data formatting | bytes 16777216 | tf_op jit(solution)/shard_map/while/body/eval_jaxpr/jit(_take)/select_n | solution.py:31
  297.2 23.7 %fusion.8 = f32[512,64,64]{2,1,0:T(8,128)} fusion(f32[512,64,64]{2,1,0:T(8,128)} %copy.41, f32[512,64,64]{2,1,0:T(8,128)} %copy.43), kind=kOutput, calls=%fused_computation.17.clone.1 | convolution fusion | flops 1610612736 | bytes 25165824 | tf_op jit(solution)/shard_map/while/body/eval_jaxpr/nik,nkj->nij/dot_general | solution.py:32
  320.9 12.7 %copy.44 = f32[512,64,64]{0,2,1:T(8,128)} copy(f32[512,64,64]{2,1,0:T(8,128)} %fusion.8) | data formatting | bytes 16777216 | tf_op jit(solution)/shard_map/while/body/eval_jaxpr/nik,nkj->nij/dot_general | solution.py:32
  333.7 8.9 %copy.45 = f32[512,4096]{1,0:T(8,128)} copy(f32[512,4096]{0,1:T(8,128)} %bitcast.50) | data formatting | bytes 16777216 | tf_op jit(solution)/shard_map/while/body/eval_jaxpr/reshape | solution.py:33
  342.6 14.2 %scatter_fusion = f32[32,4096]{1,0:T(8,128)S(1)} fusion(f32[32,4096]{1,0:T(8,128)S(1)} %get-tuple-element.185, s32[512]{0:T(512)S(1)} %bitcast.55, f32[512,4096]{1,0:T(8,128)} %copy.45), kind=kCustom, calls=%fused_computation.2.clone.1 | custom fusion | flops 2097152 | bytes 25167872 | tf_op jit(solution)/shard_map/while/body/eval_jaxpr/scatter-add | solution.py:33
  356.8 0.1 compare_select_fusion.6
  357.0 5.1 gather_fusion.1
  362.0 9.0 %copy.42 = f32[512,4096]{0,1:T(8,128)} copy(f32[512,4096]{1,0:T(8,128)} %gather_fusion.1) | data formatting | bytes 16777216 | tf_op jit(solution)/shard_map/while/body/eval_jaxpr/jit(_take)/gather | solution.py:31
  371.1 8.5 %broadcast_select_fusion.5 = f32[512,64,64]{0,2,1:T(8,128)} fusion(f32[512,64,64]{0,2,1:T(8,128)} %bitcast.51, pred[512]{0:T(512)(128)(4,1)S(1)} %compare_and_fusion.5), kind=kLoop, calls=%fused_computation.3.clone.1 | loop fusion | flops 2097152 | bytes 16777728 | tf_op jit(solution)/shard_map/while/body/eval_jaxpr/jit(_take)/select_n | solution.py:31
  379.6 11.0 %gather_fusion = f32[512,4096]{1,0:T(8,128)} fusion(f32[256,4096]{1,0:T(8,128)} %get-tuple-element.198, s32[1024]{0:T(1024)S(1)} %pad_clamp_fusion.4), kind=kCustom, calls=%fused_computation.clone.1 | custom fusion | bytes 16779264 | tf_op jit(solution)/shard_map/while/body/eval_jaxpr/jit(_take)/gather | solution.py:30
  390.6 9.0 %copy.40 = f32[512,4096]{0,1:T(8,128)} copy(f32[512,4096]{1,0:T(8,128)} %gather_fusion) | data formatting | bytes 16777216 | tf_op jit(solution)/shard_map/while/body/eval_jaxpr/jit(_take)/gather | solution.py:30
  399.6 8.5 %broadcast_select_fusion.4 = f32[512,64,64]{0,2,1:T(8,128)} fusion(f32[512,64,64]{0,2,1:T(8,128)} %bitcast.52, pred[512]{0:T(512)(128)(4,1)S(1)} %compare_and_fusion.4), kind=kLoop, calls=%fused_computation.4.clone.1 | loop fusion | flops 2097152 | bytes 16777728 | tf_op jit(solution)/shard_map/while/body/eval_jaxpr/jit(_take)/select_n | solution.py:30
  408.1 16.3 %copy.41 = f32[512,64,64]{2,1,0:T(8,128)} copy(f32[512,64,64]{0,2,1:T(8,128)} %broadcast_select_fusion.4) | data formatting | bytes 16777216 | tf_op jit(solution)/shard_map/while/body/eval_jaxpr/jit(_take)/select_n | solution.py:30
  424.4 16.2 %copy.43 = f32[512,64,64]{2,1,0:T(8,128)} copy(f32[512,64,64]{0,2,1:T(8,128)} %broadcast_select_fusion.5) | data formatting | bytes 16777216 | tf_op jit(solution)/shard_map/while/body/eval_jaxpr/jit(_take)/select_n | solution.py:31
  440.6 23.7 %fusion.8 = f32[512,64,64]{2,1,0:T(8,128)} fusion(f32[512,64,64]{2,1,0:T(8,128)} %copy.41, f32[512,64,64]{2,1,0:T(8,128)} %copy.43), kind=kOutput, calls=%fused_computation.17.clone.1 | convolution fusion | flops 1610612736 | bytes 25165824 | tf_op jit(solution)/shard_map/while/body/eval_jaxpr/nik,nkj->nij/dot_general | solution.py:32
  464.3 12.7 %copy.44 = f32[512,64,64]{0,2,1:T(8,128)} copy(f32[512,64,64]{2,1,0:T(8,128)} %fusion.8) | data formatting | bytes 16777216 | tf_op jit(solution)/shard_map/while/body/eval_jaxpr/nik,nkj->nij/dot_general | solution.py:32
  477.1 8.9 %copy.45 = f32[512,4096]{1,0:T(8,128)} copy(f32[512,4096]{0,1:T(8,128)} %bitcast.50) | data formatting | bytes 16777216 | tf_op jit(solution)/shard_map/while/body/eval_jaxpr/reshape | solution.py:33
  486.0 14.2 %scatter_fusion = f32[32,4096]{1,0:T(8,128)S(1)} fusion(f32[32,4096]{1,0:T(8,128)S(1)} %get-tuple-element.185, s32[512]{0:T(512)S(1)} %bitcast.55, f32[512,4096]{1,0:T(8,128)} %copy.45), kind=kCustom, calls=%fused_computation.2.clone.1 | custom fusion | flops 2097152 | bytes 25167872 | tf_op jit(solution)/shard_map/while/body/eval_jaxpr/scatter-add | solution.py:33
  500.2 0.1 compare_select_fusion.6
  500.4 5.1 gather_fusion.1
  505.4 9.0 %copy.42 = f32[512,4096]{0,1:T(8,128)} copy(f32[512,4096]{1,0:T(8,128)} %gather_fusion.1) | data formatting | bytes 16777216 | tf_op jit(solution)/shard_map/while/body/eval_jaxpr/jit(_take)/gather | solution.py:31
  514.5 8.5 %broadcast_select_fusion.5 = f32[512,64,64]{0,2,1:T(8,128)} fusion(f32[512,64,64]{0,2,1:T(8,128)} %bitcast.51, pred[512]{0:T(512)(128)(4,1)S(1)} %compare_and_fusion.5), kind=kLoop, calls=%fused_computation.3.clone.1 | loop fusion | flops 2097152 | bytes 16777728 | tf_op jit(solution)/shard_map/while/body/eval_jaxpr/jit(_take)/select_n | solution.py:31
  523.0 11.0 %gather_fusion = f32[512,4096]{1,0:T(8,128)} fusion(f32[256,4096]{1,0:T(8,128)} %get-tuple-element.198, s32[1024]{0:T(1024)S(1)} %pad_clamp_fusion.4), kind=kCustom, calls=%fused_computation.clone.1 | custom fusion | bytes 16779264 | tf_op jit(solution)/shard_map/while/body/eval_jaxpr/jit(_take)/gather | solution.py:30
  534.0 9.0 %copy.40 = f32[512,4096]{0,1:T(8,128)} copy(f32[512,4096]{1,0:T(8,128)} %gather_fusion) | data formatting | bytes 16777216 | tf_op jit(solution)/shard_map/while/body/eval_jaxpr/jit(_take)/gather | solution.py:30
  543.0 8.5 %broadcast_select_fusion.4 = f32[512,64,64]{0,2,1:T(8,128)} fusion(f32[512,64,64]{0,2,1:T(8,128)} %bitcast.52, pred[512]{0:T(512)(128)(4,1)S(1)} %compare_and_fusion.4), kind=kLoop, calls=%fused_computation.4.clone.1 | loop fusion | flops 2097152 | bytes 16777728 | tf_op jit(solution)/shard_map/while/body/eval_jaxpr/jit(_take)/select_n | solution.py:30
  551.5 16.3 %copy.41 = f32[512,64,64]{2,1,0:T(8,128)} copy(f32[512,64,64]{0,2,1:T(8,128)} %broadcast_select_fusion.4) | data formatting | bytes 16777216 | tf_op jit(solution)/shard_map/while/body/eval_jaxpr/jit(_take)/select_n | solution.py:30
  567.8 16.2 %copy.43 = f32[512,64,64]{2,1,0:T(8,128)} copy(f32[512,64,64]{0,2,1:T(8,128)} %broadcast_select_fusion.5) | data formatting | bytes 16777216 | tf_op jit(solution)/shard_map/while/body/eval_jaxpr/jit(_take)/select_n | solution.py:31
  584.0 23.7 %fusion.8 = f32[512,64,64]{2,1,0:T(8,128)} fusion(f32[512,64,64]{2,1,0:T(8,128)} %copy.41, f32[512,64,64]{2,1,0:T(8,128)} %copy.43), kind=kOutput, calls=%fused_computation.17.clone.1 | convolution fusion | flops 1610612736 | bytes 25165824 | tf_op jit(solution)/shard_map/while/body/eval_jaxpr/nik,nkj->nij/dot_general | solution.py:32
  607.7 12.7 %copy.44 = f32[512,64,64]{0,2,1:T(8,128)} copy(f32[512,64,64]{2,1,0:T(8,128)} %fusion.8) | data formatting | bytes 16777216 | tf_op jit(solution)/shard_map/while/body/eval_jaxpr/nik,nkj->nij/dot_general | solution.py:32
  620.5 8.9 %copy.45 = f32[512,4096]{1,0:T(8,128)} copy(f32[512,4096]{0,1:T(8,128)} %bitcast.50) | data formatting | bytes 16777216 | tf_op jit(solution)/shard_map/while/body/eval_jaxpr/reshape | solution.py:33
  629.4 14.2 %scatter_fusion = f32[32,4096]{1,0:T(8,128)S(1)} fusion(f32[32,4096]{1,0:T(8,128)S(1)} %get-tuple-element.185, s32[512]{0:T(512)S(1)} %bitcast.55, f32[512,4096]{1,0:T(8,128)} %copy.45), kind=kCustom, calls=%fused_computation.2.clone.1 | custom fusion | flops 2097152 | bytes 25167872 | tf_op jit(solution)/shard_map/while/body/eval_jaxpr/scatter-add | solution.py:33
  643.6 0.8 copy-done
  644.4 0.0 reduce-scatter.2.cloned.1.call-update
  644.4 21.8 %reduce-scatter.2.cloned.1.call-done = f32[8,4096]{1,0:T(8,128)} async-done(((f32[32,4096]{1,0:T(8,128)}), f32[8,4096]{1,0:T(8,128)}) %reduce-scatter.2.cloned.1.call-update) | async-done | bytes 131088 | tf_op jit(solution)/shard_map/reduce_scatter | solution.py:36
  (21 shorter events, 0.2 us)
Async XLA Ops:
  6.5 40.6 %all-gather.3.cloned.1.call-start = ((), (), s32[]{:S(2)}) async-start(), calls=%async_computation.2 | async-start | bytes 5242880 | tf_op jit(solution)/shard_map/all_gather | solution.py:20
  9.8 656.4 %reduce-scatter.2.cloned.1.call-start = ((), (), s32[]{:S(2)}) async-start(), calls=%async_computation.1 | async-start | bytes 655360 | tf_op jit(solution)/shard_map/reduce_scatter | solution.py:36
  57.4 12.4 %copy-start.1 = (f32[1,64,4096]{2,1,0:T(8,128)S(1)}, f32[1,64,4096]{2,1,0:T(8,128)}, u32[]{:S(2)}) copy-start(f32[1,64,4096]{2,1,0:T(8,128)} %param.4) | copy-start | bytes 3145732
  643.6 0.8 copy-start
Sparse Core Ops, SparseCore 0:
  10.0 37.1 all-gather.2
  644.5 21.6 reduce-scatter.1
where the time goes:
time: 679 us; the launch traced here: 673 us
  local copies, waits for them, and re-layouts  381 us (56%)
  other arithmetic  125 us (18%)
  matrix products  95 us (14%)
  waiting for transfers between devices  58.4 us (9%)
  between operations  13.4 us (2%)
    dot_general x4, matrix products, advance(): jnp.einsum('nik,nkj->nij', left, right, precision=lax.Precision.HIGHEST)  95 us
    gather x8, local copies, waits for them, and re-layouts, advance(): left = jnp.take(turned_panel, chosen[0], axis=0).reshape(span, BLK, BLK)  80 us
    select_n x4, local copies, waits for them, and re-layouts, advance(): left = jnp.take(turned_panel, chosen[0], axis=0).reshape(span, BLK, BLK)  65.1 us
    select_n x4, local copies, waits for them, and re-layouts, advance(): right = jnp.take(own_blocks, chosen[1], axis=0).reshape(span, BLK, BLK)  65 us
    scatter-add x4, other arithmetic, advance(): return partial_sums.at[chosen[2]].add(result.reshape(span, BB), mode='drop')  56.7 us
    gather x8, local copies, waits for them, and re-layouts, advance(): right = jnp.take(own_blocks, chosen[1], axis=0).reshape(span, BLK, BLK)  56.4 us
    dot_general x4, local copies, waits for them, and re-layouts, advance(): jnp.einsum('nik,nkj->nij', left, right, precision=lax.Precision.HIGHEST)  51 us
    all_gather x1, waiting for transfers between devices, per_device(): row_panel = lax.all_gather(own_blocks, 'row', axis=0, tiled=True)  36.5 us
  transfers between devices with their start and end apart: 2, of which 2 were waited for; matrix products, arithmetic and copies ran while one was open for 0% of the time, Pallas kernels for 0%

commit v1 on v0

v1 whole, which is shorter than its diff:
```python
import functools

import jax
import jax.numpy as jnp
from jax import lax
from jax.experimental import pallas as pl
from jax.experimental.pallas import tpu as pltpu
from jax.sharding import PartitionSpec as P

BLK = 64
BB = 4096
SC = 8
HALF = 32
LANES = 128
GROUP = 4
UNROLL = 8
CHUNKS = (32, 32)
HEAD = 128
MIB = 1 << 20


def rows_view(blocks):
    count = blocks.shape[0]
    tiles = blocks.reshape(count // 8, 8, HALF, LANES)
    return tiles.transpose(0, 2, 1, 3).reshape(count * HALF, LANES)


def blocks_view(rows):
    count = rows.shape[0] // HALF
    tiles = rows.reshape(count // 8, HALF, 8, LANES)
    return tiles.transpose(0, 2, 1, 3).reshape(count, BB)


def block_rows(ref, slot):
    start = (slot // 8) * (8 * HALF) + slot % 8
    return ref[pl.ds(start, HALF, stride=8), :]


def high_low(rows):
    high = rows.astype(jnp.bfloat16)
    low = (rows - high.astype(jnp.float32)).astype(jnp.bfloat16)
    return high, low


def fill_right(source, right, first_block, count):
    def one(slot, carry):
        high, low = high_low(block_rows(source, slot))
        at = pl.ds(pl.multiple_of((first_block + slot) * HALF, HALF), HALF)
        right[at, :LANES] = high
        right[at, LANES:] = low
        return carry

    lax.fori_loop(0, count, one, 0, unroll=8)


def fill_left(source, left, count):
    def one(slot, carry):
        high, low = high_low(block_rows(source, slot))
        high, low = high.astype(jnp.float32), low.astype(jnp.float32)
        turned = jnp.concatenate([high, low, high, low], axis=0).T
        at = pl.ds(pl.multiple_of(slot * LANES, LANES), LANES)
        left[at, :] = turned.astype(jnp.bfloat16)
        return carry

    lax.fori_loop(0, count, one, 0, unroll=2)
    left[pl.ds(count * LANES, LANES), :] = jnp.zeros((LANES, LANES), jnp.bfloat16)


def run_groups(meta, phase, code_at, empty, left, right, sums):
    begin, end = meta[phase], meta[phase + 1]
    near = lax.broadcasted_iota(jnp.int32, (LANES, LANES), 1) < BLK

    def step(number, carry):
        for inner in range(UNROLL):
            place = begin + number * UNROLL + inner
            group = meta[HEAD + place]
            base = group >> 11
            live = jnp.where(place < end, (group >> 8) & 7, 0)
            target = group & 255
            lefts, rights = [], []
            for item in range(GROUP):
                code = meta[code_at + base + item]
                own = jnp.where(item < live, code & 63, empty)
                other = jnp.where(item < live, (code >> 6) & 127, 0)
                lefts.append(left[pl.ds(pl.multiple_of(own * LANES, LANES), LANES), :])
                block = right[pl.ds(pl.multiple_of(other * HALF, HALF), HALF), :]
                rights += [block, block]
            stacked = jnp.concatenate(
                [jnp.where(near, lefts[0], lefts[1]), jnp.where(near, lefts[2], lefts[3])],
                axis=1,
            )
            term = jnp.dot(
                stacked, jnp.concatenate(rights, axis=0), preferred_element_type=jnp.float32
            )
            at = pl.ds(pl.multiple_of(target * LANES, LANES), LANES)
            sums[at, :] += term[:, :LANES] + term[:, LANES:]
        return carry

    lax.fori_loop(0, (end - begin + UNROLL - 1) // UNROLL, step, 0)


def clear(sums):
    def one(number, carry):
        at = pl.ds(pl.multiple_of(number * LANES, LANES), LANES)
        sums[at, :] = jnp.zeros((LANES, LANES), jnp.float32)
        return carry

    lax.fori_loop(0, sums.shape[0] // LANES, one, 0, unroll=2)


def pack_pairs(sums, earlier, outs):
    near = lax.broadcasted_iota(jnp.int32, (BLK, LANES), 1) < BLK
    for turn, out in enumerate(outs):
        for pair in range(SC // 2):
            at = (turn * SC + 2 * pair) * LANES
            upper0 = sums[at : at + BLK, :]
            lower0 = sums[at + BLK : at + LANES, :]
            upper1 = sums[at + LANES : at + LANES + BLK, :]
            lower1 = sums[at + LANES + BLK : at + 2 * LANES, :]
            one = upper0 + pltpu.roll(lower0, BLK, 1)
            two = pltpu.roll(upper1, BLK, 1) + lower1
            both = jnp.where(near, one, two)
            if earlier is not None:
                both = both + earlier[turn][pair]
            out[pair] = both


def near_kernel(turns, code_at, meta, own, sibling, left, *rest):
    outs, (right, sums) = rest[:turns], rest[turns:]
    count = own.shape[0] // HALF
    fill_left(own, left, count)
    fill_right(own, right, 0, count)
    fill_right(sibling, right, count, count)
    clear(sums)
    run_groups(meta, 0, code_at, count, left, right, sums)
    pack_pairs(sums, None, outs)


def far_kernel(turns, code_at, phase, meta, straight, crossed, left, *rest):
    earlier, outs, (right, sums) = rest[:turns], rest[turns : 2 * turns], rest[2 * turns :]
    count = straight.shape[0] // HALF
    fill_right(straight, right, 0, count)
    fill_right(crossed, right, count, count)
    clear(sums)
    empty = left.shape[0] // LANES - 1
    run_groups(meta, phase, code_at, empty, left, right, sums)
    pack_pairs(sums, earlier, outs)


def last_kernel(*refs):
    parts, out, turned = refs[:-2], refs[-2], refs[-1]
    for pair in range(SC // 2):
        total = parts[0][pair]
        for part in parts[1:]:
            total = total + part[pair]
        turned[:, :BLK] = total.T
        even = turned[pl.ds(0, BLK, stride=2), :]
        odd = turned[pl.ds(1, BLK, stride=2), :]
        near = lax.broadcasted_iota(jnp.int32, (BLK, LANES), 1) < BLK
        packed = jnp.where(near, even, pltpu.roll(odd, BLK, 1))
        out[pl.ds(2 * pair, HALF, stride=8), :] = packed[:HALF]
        out[pl.ds(2 * pair + 1, HALF, stride=8), :] = packed[HALF:]


def plan(lists, slots, row, col, columns, chips):
    first, second, target = lists[0], lists[1], lists[2]
    entries = first.shape[0]
    targets = columns * SC
    phases = 1 + (chips - 1) * len(CHUNKS)
    shard, slot = first // slots, first % slots
    hop = (shard // 2 - row // 2) % chips
    crossed = (shard ^ row) & 1
    chunk = jnp.zeros_like(slot)
    start = jnp.zeros_like(slot)
    size = jnp.full_like(slot, CHUNKS[0])
    at = 0
    for number, width in enumerate(CHUNKS):
        inside = slot >= at
        chunk = jnp.where(inside, number, chunk)
        start = jnp.where(inside, at, start)
        size = jnp.where(inside, width, size)
        at += width
    close = hop == 0
    phase = jnp.where(close, 0, 1 + (hop - 1) * len(CHUNKS) + chunk)
    panel_slot = jnp.where(close, crossed * slots + slot, crossed * size + slot - start)
    turn = (target // SC - col) % columns
    segments = phases * targets
    segment = jnp.where(target < targets, phase * targets + turn * SC + target % SC, segments)
    codes = lax.sort((segment << 13) | (panel_slot << 6) | second)

    edges = jnp.arange(segments + 1)
    sorted_segment = codes >> 13
    starts = jnp.sum((sorted_segment[None, :] < edges[:, None]).astype(jnp.int32), axis=1)
    live = starts[1:] - starts[:-1]
    groups = (live + GROUP - 1) // GROUP
    upto = edges[:-1][None, :] < edges[:, None]
    group_starts = jnp.sum(jnp.where(upto, groups[None, :], 0), axis=1)

    places = -(-(entries // GROUP + segments + UNROLL) // LANES) * LANES
    place = jnp.arange(places)
    passed = group_starts[1:][None, :] <= place[:, None]
    shift = starts - GROUP * group_starts
    in_segment = jnp.sum(passed.astype(jnp.int32), axis=1)
    offset = shift[0] + jnp.sum(jnp.where(passed, (shift[1:] - shift[:-1])[None, :], 0), axis=1)
    stops = jnp.concatenate([starts[1:], starts[-1:]])
    stop = stops[0] + jnp.sum(jnp.where(passed, (stops[1:] - stops[:-1])[None, :], 0), axis=1)
    base = jnp.clip(GROUP * place + offset, 0, entries)
    valid = jnp.clip(stop - base, 0, GROUP)
    described = (base << 11) | (valid << 8) | (in_segment % targets)

    bounds = group_starts[::targets]
    meta = jnp.concatenate(
        [
            jnp.pad(bounds, (0, HEAD - bounds.shape[0])),
            described,
            codes,
            jnp.zeros((LANES,), jnp.int32),
        ]
    )
    return meta, HEAD + places


def per_device(columns, rows, p_blocks, products):
    own_blocks = p_blocks[0]
    slots = own_blocks.shape[0]
    chips = rows // 2
    targets = columns * SC
    row, col = lax.axis_index("row"), lax.axis_index("col")
    swap = [(device, device ^ 1) for device in range(rows)]

    far = []
    for hop in range(1, chips):
        jump = [((device + 2 * hop) % rows, device) for device in range(rows)]
        at = 0
        for width in CHUNKS:
            piece = own_blocks[at : at + width]
            at += width
            straight = lax.ppermute(piece, "row", jump)
            far.append((straight, lax.ppermute(straight, "row", swap)))
    sibling = lax.ppermute(own_blocks, "row", swap)

    meta, code_at = plan(products[0, 0], slots, row, col, columns, chips)
    smem = pl.BlockSpec(memory_space=pltpu.SMEM)
    vmem = pl.BlockSpec(memory_space=pltpu.VMEM)
    part = jax.ShapeDtypeStruct((SC // 2, BLK, LANES), jnp.float32)
    sums_size = targets * LANES * LANES * 4
    left_shape = jax.ShapeDtypeStruct(((slots + 1) * LANES, LANES), jnp.bfloat16)
    sums = pltpu.VMEM((targets * LANES, LANES), jnp.float32)

    left, *parts = pl.pallas_call(
        functools.partial(near_kernel, columns, code_at),
        in_specs=[smem, vmem, vmem],
        out_specs=[vmem] * (1 + columns),
        out_shape=[left_shape] + [part] * columns,
        scratch_shapes=[pltpu.VMEM((2 * slots * HALF, 2 * LANES), jnp.bfloat16), sums],
        compiler_params=pltpu.CompilerParams(vmem_limit_bytes=16 * MIB + 2 * sums_size),
        cost_estimate=pl.CostEstimate(flops=20_000_000_000, bytes_accessed=8 * MIB, transcendentals=0),
    )(meta, rows_view(own_blocks), rows_view(sibling))

    for number, (straight, crossed) in enumerate(far):
        width = straight.shape[0]
        parts = pl.pallas_call(
            functools.partial(far_kernel, columns, code_at, 1 + number),
            in_specs=[smem] + [vmem] * (3 + columns),
            out_specs=[vmem] * columns,
            out_shape=[part] * columns,
            scratch_shapes=[pltpu.VMEM((2 * width * HALF, 2 * LANES), jnp.bfloat16), sums],
            compiler_params=pltpu.CompilerParams(vmem_limit_bytes=16 * MIB + 2 * sums_size),
            cost_estimate=pl.CostEstimate(flops=8_000_000_000, bytes_accessed=6 * MIB, transcendentals=0),
        )(meta, rows_view(straight), rows_view(crossed), left, *parts)

    arrived = [parts[0]]
    for turn in range(1, columns):
        ahead = [(device, (device + turn) % columns) for device in range(columns)]
        arrived.append(lax.ppermute(parts[turn], "col", ahead))

    owned = pl.pallas_call(
        last_kernel,
        in_specs=[vmem] * columns,
        out_specs=vmem,
        out_shape=jax.ShapeDtypeStruct((SC * HALF, LANES), jnp.float32),
        scratch_shapes=[pltpu.VMEM((LANES, LANES), jnp.float32)],
        compiler_params=pltpu.CompilerParams(vmem_limit_bytes=16 * MIB),
    )(*arrived)
    return blocks_view(owned)[None]


def solution(mesh):
    columns, rows = mesh.shape["col"], mesh.shape["row"]
    return jax.shard_map(
        functools.partial(per_device, columns, rows),
        mesh=mesh,
        in_specs=(P(("groups", "col"), "row", None), P(("groups", "col"), "row", None, None)),
        out_specs=P(("groups", "row"), "col", None),
        check_vma=False,
    )
```

time: 679 us -> 74.2 us (0.11)
  the two profiles are of different devices: /device:TPU:0 before, /device:TPU:11 now
where the time goes in v1:
time: 74.2 us; the launch traced here: 74 us
  Pallas kernels  26.3 us (35%)
  waiting for transfers between devices  22.7 us (31%)
  starting transfers between devices  14.5 us (20%)
  other arithmetic  7.11 us (10%)
  local copies, waits for them, and re-layouts  3.19 us (4%)
    ppermute x2, waiting for transfers between devices, per_device(): straight = lax.ppermute(piece, 'row', jump)  14 us
    pallas_call x1, Pallas kernels, per_device(): pl.pallas_call(functools.partial(near_kernel, columns, code_at), in_specs...  13.6 us
    pallas_call x2, Pallas kernels, per_device(): pl.pallas_call(functools.partial(far_kernel, columns, code_at, 1 + number...  11.8 us
    ppermute x3, starting transfers between devices, per_device(): arrived.append(lax.ppermute(parts[turn], 'col', ahead))  10.2 us
    ppermute x3, waiting for transfers between devices, per_device(): arrived.append(lax.ppermute(parts[turn], 'col', ahead))  8.66 us
    sort x1, other arithmetic, plan(): codes = lax.sort(segment << 13 | panel_slot << 6 | second)  5.04 us
    slice x1, local copies, waits for them, and re-layouts, per_device(): piece = own_blocks[at:at + width]  2.26 us
    ppermute x2, starting transfers between devices, per_device(): far.append((straight, lax.ppermute(straight, 'row', swap)))  2.22 us
  transfers between devices with their start and end apart: 8, of which 4 were waited for; matrix products, arithmetic and copies ran while one was open for 14% of the time, Pallas kernels for 27%

profile of v1, /device:TPU:11, one launch (start us, length us, event | category | flops | bytes accessed | tf_op | source)
XLA Modules:
  0.0 74.0 jit_solution(7493399107430505582)
XLA Ops:
  0.0 0.0 copy-start
  0.0 0.0 copy-start.1
  0.0 0.7 collective-permute-start.2
  0.7 2.3 %slice_bitcast_fusion = (f32[32,4096]{1,0:T(8,128)}, f32[32,4096]{1,0:T(8,128)}) fusion(f32[1,64,4096]{2,1,0:T(8,128)} %param.2), kind=kLoop, calls=%fused_computation.2 | loop fusion | bytes 2097152 | tf_op jit(solution)/shard_map/slice | solution.py:236
  2.9 0.3 collective-permute-start.3
  3.2 1.2 %collective-permute-start = (f32[32,4096]{1,0:T(8,128)}, f32[32,4096]{1,0:T(8,128)S(1)}, u32[]{:S(2)}, u32[]{:S(2)}) collective-permute-start(f32[32,4096]{1,0:T(8,128)} %get-tuple-element.38), channel_id=1, source_target_pairs={{2,0},{3,1},{0,2},{1,3},{6,4},{7,5},{4,6},{5,7},{10,8},{11,9},{8,1... | collective-permute-start | bytes 1572872 | tf_op jit(solution)/shard_map/ppermute | solution.py:238
  4.4 0.0 copy-done.1
  4.5 5.0 %sort.14 = (s32[2048]{0:T(1024)S(1)}, s32[2048]{0:T(1024)}) sort(s32[2048]{0:T(1024)S(1)} %fusion.13, s32[2048]{0:T(1024)S(1)} %iota.17), dimensions={0}, to_apply=%region_0.1 | sort | flops 22528 | bytes 32768 | tf_op jit(solution)/shard_map/sort | solution.py:189
  9.5 0.2 convert_reduce_fusion
  9.7 0.7 fusion.20
  10.4 0.1 slice.63
  10.5 0.8 %pad_add_fusion.1 = s32[97]{0:T(128)S(1)} fusion(s32[1]{0:T(128)} %get-tuple-element.43, s32[96]{0:T(128)S(1)} %slice.63), kind=kLoop, calls=%fused_computation.61 | loop fusion | flops 97 | bytes 776 | tf_op jit(solution)/shard_map/concatenate | solution.py:205
  11.2 0.1 slice_subtract_fusion
  11.3 0.1 select_reduce_fusion.2
  11.4 0.1 slice_subtract_fusion.1
  11.5 0.1 slice.67
  11.6 0.1 slice.65
  11.7 0.1 convert_reduce_fusion.1
  11.8 0.7 fusion.18
  12.5 4.1 %collective-permute-done.3 = f32[32,4096]{1,0:T(8,128)S(1)} collective-permute-done((f32[32,4096]{1,0:T(8,128)}, f32[32,4096]{1,0:T(8,128)S(1)}, u32[]{:S(2)}, u32[]{:S(2)}) %collective-permute-start.3) | collective-permute-done | bytes 524320 | tf_op jit(solution)/shard_map/ppermute | solution.py:238
  16.6 1.3 %collective-permute-start.4 = (f32[32,4096]{1,0:T(8,128)S(1)}, f32[32,4096]{1,0:T(8,128)S(1)}, u32[]{:S(2)}, u32[]{:S(2)}) collective-permute-start(f32[32,4096]{1,0:T(8,128)S(1)} %collective-permute-done.3), channel_id=1, source_target_pairs={{0,1},{1,0},{2,3},{3,2},{4,5},{5,4},{6,7},{7,6},{8,9},{9,8},{10,11... | collective-permute-start | bytes 1572872 | tf_op jit(solution)/shard_map/ppermute | solution.py:239
  18.0 9.9 %collective-permute-done = f32[32,4096]{1,0:T(8,128)S(1)} collective-permute-done((f32[32,4096]{1,0:T(8,128)}, f32[32,4096]{1,0:T(8,128)S(1)}, u32[]{:S(2)}, u32[]{:S(2)}) %collective-permute-start) | collective-permute-done | bytes 524320 | tf_op jit(solution)/shard_map/ppermute | solution.py:238
  27.9 0.9 %collective-permute-start.1 = (f32[32,4096]{1,0:T(8,128)S(1)}, f32[32,4096]{1,0:T(8,128)S(1)}, u32[]{:S(2)}, u32[]{:S(2)}) collective-permute-start(f32[32,4096]{1,0:T(8,128)S(1)} %collective-permute-done), channel_id=1, source_target_pairs={{0,1},{1,0},{2,3},{3,2},{4,5},{5,4},{6,7},{7,6},{8,9},{9,8},{10,11... | collective-permute-start | bytes 1572872 | tf_op jit(solution)/shard_map/ppermute | solution.py:239
  28.8 0.0 collective-permute-done.2
  28.8 0.0 copy-done
  28.8 13.6 %shard_map.28 = (bf16[8320,128]{1,0:T(8,128)(2,1)S(1)}, f32[4,64,128]{2,1,0:T(8,128)S(1)}, f32[4,64,128]{2,1,0:T(8,128)S(1)}, f32[4,64,128]{2,1,0:T(8,128)S(1)}, f32[4,64,128]{2,1,0:T(8,128)S(1)}) custom-call(s32[2944]{0:T(1024)S(1)} %fusion.1.meta, f32[2048,128]{1,0:T(8,128)S(1)} %bitcast.48, f32[2048,128]{1,0:T(8,128)S(1)} %bitcast.49), custom_call_target="tpu_custom_call" | custom-call | flops 20000000000 | bytes 8388608 | tf_op jit(solution)/shard_map/pallas_call | solution.py:250
  42.3 0.0 collective-permute-done.4
  42.3 6.1 %shard_map.29 = (f32[4,64,128]{2,1,0:T(8,128)S(1)}, f32[4,64,128]{2,1,0:T(8,128)S(1)}, f32[4,64,128]{2,1,0:T(8,128)S(1)}, f32[4,64,128]{2,1,0:T(8,128)S(1)}) custom-call(s32[2944]{0:T(1024)S(1)} %fusion.1.meta, f32[1024,128]{1,0:T(8,128)S(1)} %bitcast.51, f32[1024,128]{1,0:T(8,128)S(1)} %bitcast.53, bf16[8320,128]{1,0:T(8,128)(2,1)S(1)} %get-tuple-element.21.left, ...), custom_call_target="tpu_custom_call" | custom-call | flops 8000000000 | bytes 6291456 | tf_op jit(solution)/shard_map/pallas_call | solution.py:262
  48.4 0.0 collective-permute-done.1
  48.5 5.7 %shard_map.30 = (f32[4,64,128]{2,1,0:T(8,128)S(1)}, f32[4,64,128]{2,1,0:T(8,128)S(1)}, f32[4,64,128]{2,1,0:T(8,128)S(1)}, f32[4,64,128]{2,1,0:T(8,128)S(1)}) custom-call(s32[2944]{0:T(1024)S(1)} %fusion.1.meta, f32[1024,128]{1,0:T(8,128)S(1)} %bitcast.50, f32[1024,128]{1,0:T(8,128)S(1)} %bitcast.52, bf16[8320,128]{1,0:T(8,128)(2,1)S(1)} %get-tuple-element.21.left, ...), custom_call_target="tpu_custom_call" | custom-call | flops 8000000000 | bytes 6291456 | tf_op jit(solution)/shard_map/pallas_call | solution.py:262
  54.2 6.3 %collective-permute-start.5 = (f32[4,64,128]{2,1,0:T(8,128)S(1)}, f32[4,64,128]{2,1,0:T(8,128)S(1)}, u32[]{:S(2)}, u32[]{:S(2)}) collective-permute-start(f32[4,64,128]{2,1,0:T(8,128)S(1)} %get-tuple-element.31), channel_id=1, source_target_pairs={{0,4},{4,8},{8,12},{12,0},{1,5},{5,9},{9,13},{13,1},{2,6},{6,10},{... | collective-permute-start | bytes 393224 | tf_op jit(solution)/shard_map/ppermute | solution.py:275
  60.5 2.5 %collective-permute-start.6 = (f32[4,64,128]{2,1,0:T(8,128)S(1)}, f32[4,64,128]{2,1,0:T(8,128)S(1)}, u32[]{:S(2)}, u32[]{:S(2)}) collective-permute-start(f32[4,64,128]{2,1,0:T(8,128)S(1)} %get-tuple-element.32), channel_id=1, source_target_pairs={{0,8},{4,12},{8,0},{12,4},{1,9},{5,13},{9,1},{13,5},{2,10},{6,14},... | collective-permute-start | bytes 393224 | tf_op jit(solution)/shard_map/ppermute | solution.py:275
  63.0 1.4 %collective-permute-start.7 = (f32[4,64,128]{2,1,0:T(8,128)S(1)}, f32[4,64,128]{2,1,0:T(8,128)S(1)}, u32[]{:S(2)}, u32[]{:S(2)}) collective-permute-start(f32[4,64,128]{2,1,0:T(8,128)S(1)} %get-tuple-element.33), channel_id=1, source_target_pairs={{0,12},{4,0},{8,4},{12,8},{1,13},{5,1},{9,5},{13,9},{2,14},{6,2},{... | collective-permute-start | bytes 393224 | tf_op jit(solution)/shard_map/ppermute | solution.py:275
  64.4 0.0 collective-permute-done.5.refs_1_
  64.4 2.9 %collective-permute-done.6.refs_2_ = f32[4,64,128]{2,1,0:T(8,128)S(1)} collective-permute-done((f32[4,64,128]{2,1,0:T(8,128)S(1)}, f32[4,64,128]{2,1,0:T(8,128)S(1)}, u32[]{:S(2)}, u32[]{:S(2)}) %collective-permute-start.6) | collective-permute-done | bytes 131104 | tf_op jit(solution)/shard_map/ppermute | solution.py:275
  67.3 5.7 %collective-permute-done.7.refs_3_ = f32[4,64,128]{2,1,0:T(8,128)S(1)} collective-permute-done((f32[4,64,128]{2,1,0:T(8,128)S(1)}, f32[4,64,128]{2,1,0:T(8,128)S(1)}, u32[]{:S(2)}, u32[]{:S(2)}) %collective-permute-start.7) | collective-permute-done | bytes 131104 | tf_op jit(solution)/shard_map/ppermute | solution.py:275
  73.0 0.9 %shard_map.31 = f32[256,128]{1,0:T(8,128)} custom-call(f32[4,64,128]{2,1,0:T(8,128)S(1)} %get-tuple-element.30.refs_0_, f32[4,64,128]{2,1,0:T(8,128)S(1)} %collective-permute-done.5.refs_1_, f32[4,64,128]{2,1,0:T(8,128)S(1)} %collective-permute-done.6.refs_2_, f32[4,64,128]{2,1,0:T(8,128)S(1)} %collective-permute-done.7.refs_3_), custom_call_target="tpu_custom_call" | custom-call | tf_op jit(solution)/shard_map/pallas_call | solution.py:277
  (8 shorter events, 0.1 us)
Async XLA Ops:
  0.0 28.8 %copy-start = (f32[1,64,4096]{2,1,0:T(8,128)S(1)}, f32[1,64,4096]{2,1,0:T(8,128)}, u32[]{:S(2)}) copy-start(f32[1,64,4096]{2,1,0:T(8,128)} %param.2) | copy-start | bytes 3145732
  0.0 4.4 %copy-start.1 = (s32[1,1,3,2048]{3,1,2,0:T(1,128)S(1)}, s32[1,1,3,2048]{3,1,2,0:T(1,128)}, u32[]{:S(2)}) copy-start(s32[1,1,3,2048]{3,1,2,0:T(1,128)} %param.3) | copy-start | bytes 73732
  0.0 28.7 %collective-permute-start.2 = (f32[64,4096]{1,0:T(8,128)}, f32[64,4096]{1,0:T(8,128)S(1)}, u32[]{:S(2)}, u32[]{:S(2)}) collective-permute-start(f32[64,4096]{1,0:T(8,128)} %bitcast.47), channel_id=1, source_target_pairs={{0,1},{1,0},{2,3},{3,2},{4,5},{5,4},{6,7},{7,6},{8,9},{9,8},{10,11... | collective-permute-start | bytes 3145736 | tf_op jit(solution)/shard_map/ppermute | solution.py:240
  2.9 13.7 %collective-permute-start.3 = (f32[32,4096]{1,0:T(8,128)}, f32[32,4096]{1,0:T(8,128)S(1)}, u32[]{:S(2)}, u32[]{:S(2)}) collective-permute-start(f32[32,4096]{1,0:T(8,128)} %get-tuple-element.37), channel_id=1, source_target_pairs={{2,0},{3,1},{0,2},{1,3},{6,4},{7,5},{4,6},{5,7},{10,8},{11,9},{8,1... | collective-permute-start | bytes 1572872 | tf_op jit(solution)/shard_map/ppermute | solution.py:238
  3.2 24.7 %collective-permute-start = (f32[32,4096]{1,0:T(8,128)}, f32[32,4096]{1,0:T(8,128)S(1)}, u32[]{:S(2)}, u32[]{:S(2)}) collective-permute-start(f32[32,4096]{1,0:T(8,128)} %get-tuple-element.38), channel_id=1, source_target_pairs={{2,0},{3,1},{0,2},{1,3},{6,4},{7,5},{4,6},{5,7},{10,8},{11,9},{8,1... | collective-permute-start | bytes 1572872 | tf_op jit(solution)/shard_map/ppermute | solution.py:238
  16.6 25.7 %collective-permute-start.4 = (f32[32,4096]{1,0:T(8,128)S(1)}, f32[32,4096]{1,0:T(8,128)S(1)}, u32[]{:S(2)}, u32[]{:S(2)}) collective-permute-start(f32[32,4096]{1,0:T(8,128)S(1)} %collective-permute-done.3), channel_id=1, source_target_pairs={{0,1},{1,0},{2,3},{3,2},{4,5},{5,4},{6,7},{7,6},{8,9},{9,8},{10,11... | collective-permute-start | bytes 1572872 | tf_op jit(solution)/shard_map/ppermute | solution.py:239
  27.9 20.6 %collective-permute-start.1 = (f32[32,4096]{1,0:T(8,128)S(1)}, f32[32,4096]{1,0:T(8,128)S(1)}, u32[]{:S(2)}, u32[]{:S(2)}) collective-permute-start(f32[32,4096]{1,0:T(8,128)S(1)} %collective-permute-done), channel_id=1, source_target_pairs={{0,1},{1,0},{2,3},{3,2},{4,5},{5,4},{6,7},{7,6},{8,9},{9,8},{10,11... | collective-permute-start | bytes 1572872 | tf_op jit(solution)/shard_map/ppermute | solution.py:239
  54.2 10.2 %collective-permute-start.5 = (f32[4,64,128]{2,1,0:T(8,128)S(1)}, f32[4,64,128]{2,1,0:T(8,128)S(1)}, u32[]{:S(2)}, u32[]{:S(2)}) collective-permute-start(f32[4,64,128]{2,1,0:T(8,128)S(1)} %get-tuple-element.31), channel_id=1, source_target_pairs={{0,4},{4,8},{8,12},{12,0},{1,5},{5,9},{9,13},{13,1},{2,6},{6,10},{... | collective-permute-start | bytes 393224 | tf_op jit(solution)/shard_map/ppermute | solution.py:275
  60.5 6.8 %collective-permute-start.6 = (f32[4,64,128]{2,1,0:T(8,128)S(1)}, f32[4,64,128]{2,1,0:T(8,128)S(1)}, u32[]{:S(2)}, u32[]{:S(2)}) collective-permute-start(f32[4,64,128]{2,1,0:T(8,128)S(1)} %get-tuple-element.32), channel_id=1, source_target_pairs={{0,8},{4,12},{8,0},{12,4},{1,9},{5,13},{9,1},{13,5},{2,10},{6,14},... | collective-permute-start | bytes 393224 | tf_op jit(solution)/shard_map/ppermute | solution.py:275
  63.0 10.1 %collective-permute-start.7 = (f32[4,64,128]{2,1,0:T(8,128)S(1)}, f32[4,64,128]{2,1,0:T(8,128)S(1)}, u32[]{:S(2)}, u32[]{:S(2)}) collective-permute-start(f32[4,64,128]{2,1,0:T(8,128)S(1)} %get-tuple-element.33), channel_id=1, source_target_pairs={{0,12},{4,0},{8,4},{12,8},{1,13},{5,1},{9,5},{13,9},{2,14},{6,2},{... | collective-permute-start | bytes 393224 | tf_op jit(solution)/shard_map/ppermute | solution.py:275

commit v2 on v1

v2 whole, which is shorter than its diff:
```python
import functools

import jax
import jax.numpy as jnp
from jax import lax
from jax.experimental import pallas as pl
from jax.experimental.pallas import tpu as pltpu
from jax.sharding import PartitionSpec as P

BLK = 64
BB = 4096
SC = 8
HALF = 32
LANES = 128
GROUP = 4
UNROLLS = (32, 8)
HEAD = 256
MIB = 1 << 20


def rows_view(blocks):
    count = blocks.shape[0]
    tiles = blocks.reshape(count // 8, 8, HALF, LANES)
    return tiles.transpose(0, 2, 1, 3).reshape(count * HALF, LANES)


def blocks_view(rows):
    count = rows.shape[0] // HALF
    tiles = rows.reshape(count // 8, HALF, 8, LANES)
    return tiles.transpose(0, 2, 1, 3).reshape(count, BB)


def block_rows(ref, slot):
    start = (slot // 8) * (8 * HALF) + slot % 8
    return ref[pl.ds(start, HALF, stride=8), :]


def high_low(rows):
    high = rows.astype(jnp.bfloat16)
    low = (rows - high.astype(jnp.float32)).astype(jnp.bfloat16)
    return high, low


def fill_right(source, right, first_block, count):
    def one(slot, carry):
        high, low = high_low(block_rows(source, slot))
        at = pl.ds(pl.multiple_of((first_block + slot) * HALF, HALF), HALF)
        right[at, :LANES] = high
        right[at, LANES:] = low
        return carry

    lax.fori_loop(0, count, one, 0, unroll=8)


def fill_left(source, left, count):
    def one(slot, carry):
        high, low = high_low(block_rows(source, slot))
        at = pl.ds(pl.multiple_of(slot * LANES, LANES), LANES)
        left[at, :] = jnp.concatenate([high, low, high, low], axis=0).T
        return carry

    lax.fori_loop(0, count, one, 0, unroll=2)
    left[pl.ds(count * LANES, LANES), :] = jnp.zeros((LANES, LANES), jnp.bfloat16)


def run_groups(meta, bounds, code_at, empty, left, right, sums):
    begin, end = meta[bounds[0]], meta[bounds[1]]
    first_target = bounds[2] * SC
    near = lax.broadcasted_iota(jnp.int32, (LANES, LANES), 1) < BLK

    def multiply(place):
        group = meta[HEAD + place]
        base = group >> 12
        live = jnp.where(place < end, (group >> 8) & 15, 0)
        target = jnp.clip((group & 255) - first_target, 0, sums.shape[0] // LANES - 1)
        lefts, rights = [], []
        for item in range(GROUP):
            code = meta[code_at + base + item]
            own = jnp.where(item < live, code & 63, empty)
            other = jnp.where(item < live, (code >> 6) & 127, 0)
            lefts.append(left[pl.ds(pl.multiple_of(own * LANES, LANES), LANES), :])
            block = right[pl.ds(pl.multiple_of(other * HALF, HALF), HALF), :]
            rights += [block, block]
        stacked = jnp.concatenate(
            [jnp.where(near, lefts[item], lefts[item + 1]) for item in range(0, GROUP, 2)],
            axis=1,
        )
        term = jnp.dot(
            stacked, jnp.concatenate(rights, axis=0), preferred_element_type=jnp.float32
        )
        at = pl.ds(pl.multiple_of(target * LANES, LANES), LANES)
        sums[at, :] += term[:, :LANES] + term[:, LANES:]

    wide, narrow = UNROLLS

    def wide_step(number, carry):
        for inner in range(wide):
            multiply(begin + number * wide + inner)
        return carry

    whole = (end - begin) // wide
    middle = begin + whole * wide

    def narrow_step(number, carry):
        for inner in range(narrow):
            multiply(middle + number * narrow + inner)
        return carry

    lax.fori_loop(0, whole, wide_step, 0)
    lax.fori_loop(0, (end - middle + narrow - 1) // narrow, narrow_step, 0)


def clear(sums):
    def one(number, carry):
        at = pl.ds(pl.multiple_of(number * LANES, LANES), LANES)
        sums[at, :] = jnp.zeros((LANES, LANES), jnp.float32)
        return carry

    lax.fori_loop(0, sums.shape[0] // LANES, one, 0, unroll=2)


def pack_pairs(sums, earlier, outs):
    near = lax.broadcasted_iota(jnp.int32, (BLK, LANES), 1) < BLK
    for place, out in enumerate(outs):
        for pair in range(SC // 2):
            at = (place * SC + 2 * pair) * LANES
            upper0 = sums[at : at + BLK, :]
            lower0 = sums[at + BLK : at + LANES, :]
            upper1 = sums[at + LANES : at + LANES + BLK, :]
            lower1 = sums[at + LANES + BLK : at + 2 * LANES, :]
            one = upper0 + pltpu.roll(lower0, BLK, 1)
            two = pltpu.roll(upper1, BLK, 1) + lower1
            both = jnp.where(near, one, two)
            if earlier:
                both = both + earlier[place][pair]
            out[pair] = both


def product_kernel(code_at, bounds, new_left, sources, earlier, keep, *refs):
    refs = list(refs)
    take = lambda count: [refs.pop(0) for _ in range(count)]
    (meta,) = take(1)
    sources = take(sources)
    left = None if new_left else take(1)[0]
    right = None if sources else take(1)[0]
    earlier = take(earlier)
    left = take(1)[0] if new_left else left
    right = take(1)[0] if keep else right
    sums = refs.pop()
    right = refs.pop() if right is None else right
    if new_left:
        fill_left(sources[0], left, sources[0].shape[0] // HALF)
    at = 0
    for source in sources:
        fill_right(source, right, at, source.shape[0] // HALF)
        at += source.shape[0] // HALF
    clear(sums)
    run_groups(meta, bounds, code_at, left.shape[0] // LANES - 1, left, right, sums)
    pack_pairs(sums, earlier, refs)


def last_kernel(*refs):
    parts, out, turned = refs[:-2], refs[-2], refs[-1]
    for pair in range(SC // 2):
        total = parts[0][pair]
        for part in parts[1:]:
            total = total + part[pair]
        turned[:, :BLK] = total.T
        even = turned[pl.ds(0, BLK, stride=2), :]
        odd = turned[pl.ds(1, BLK, stride=2), :]
        near = lax.broadcasted_iota(jnp.int32, (BLK, LANES), 1) < BLK
        packed = jnp.where(near, even, pltpu.roll(odd, BLK, 1))
        out[pl.ds(2 * pair, HALF, stride=8), :] = packed[:HALF]
        out[pl.ds(2 * pair + 1, HALF, stride=8), :] = packed[HALF:]


def sent_order(columns):
    groups = [list(range(2, columns - 1)), sorted({1, columns - 1} - {0}), [0]]
    return [turns for turns in groups if turns]


def plan(lists, slots, row, col, columns, chips):
    first, second, target = lists[0], lists[1], lists[2]
    entries = first.shape[0]
    targets = columns * SC
    phases = 2 * chips - 1
    shard, slot = first // slots, first % slots
    hop = (shard // 2 - row // 2) % chips
    crossed = (shard ^ row) & 1
    close = hop == 0
    phase = jnp.where(close, 0, 2 * hop - 1 + crossed)
    panel_slot = jnp.where(close, crossed * slots + slot, slot)
    turn = (target // SC - col) % columns
    position = turn
    for number, one in enumerate(sum(sent_order(columns), [])):
        position = jnp.where(turn == one, number, position)
    segments = phases * targets
    segment = jnp.where(target < targets, phase * targets + position * SC + target % SC, segments)
    codes = lax.sort((segment << 13) | (panel_slot << 6) | second)

    edges = jnp.arange(segments + 1)
    sorted_segment = codes >> 13
    starts = jnp.sum((sorted_segment[None, :] < edges[:, None]).astype(jnp.int32), axis=1)
    live = starts[1:] - starts[:-1]
    groups = (live + GROUP - 1) // GROUP
    upto = edges[:-1][None, :] < edges[:, None]
    group_starts = jnp.sum(jnp.where(upto, groups[None, :], 0), axis=1)

    places = -(-(entries // GROUP + segments + UNROLLS[0]) // LANES) * LANES
    place = jnp.arange(places)
    passed = group_starts[1:][None, :] <= place[:, None]
    shift = starts - GROUP * group_starts
    in_segment = jnp.sum(passed.astype(jnp.int32), axis=1)
    offset = shift[0] + jnp.sum(jnp.where(passed, (shift[1:] - shift[:-1])[None, :], 0), axis=1)
    stops = jnp.concatenate([starts[1:], starts[-1:]])
    stop = stops[0] + jnp.sum(jnp.where(passed, (stops[1:] - stops[:-1])[None, :], 0), axis=1)
    base = jnp.clip(GROUP * place + offset, 0, entries)
    valid = jnp.clip(stop - base, 0, GROUP)
    described = (base << 12) | (valid << 8) | (in_segment % targets)

    bounds = group_starts[::SC]
    meta = jnp.concatenate(
        [
            jnp.pad(bounds, (0, HEAD - bounds.shape[0])),
            described,
            codes,
            jnp.zeros((LANES,), jnp.int32),
        ]
    )
    return meta, HEAD + places


def products_of(meta, code_at, columns, phase, places, sources, left, right, earlier, keep=False):
    smem = pl.BlockSpec(memory_space=pltpu.SMEM)
    vmem = pl.BlockSpec(memory_space=pltpu.VMEM)
    part = jax.ShapeDtypeStruct((SC // 2, BLK, LANES), jnp.float32)
    first, last = places
    new_left = left is None
    out_shape = [part] * (last - first)
    slots = sources[0].shape[0] if sources else right.shape[0] // HALF
    right_shape = (max(len(sources), 1) * slots * HALF, 2 * LANES)
    if keep:
        out_shape = [jax.ShapeDtypeStruct(right_shape, jnp.bfloat16)] + out_shape
    if new_left:
        left_shape = ((slots + 1) * LANES, LANES)
        out_shape = [jax.ShapeDtypeStruct(left_shape, jnp.bfloat16)] + out_shape
    scratch = [pltpu.VMEM(((last - first) * SC * LANES, LANES), jnp.float32)]
    if sources and not keep:
        scratch = [pltpu.VMEM(right_shape, jnp.bfloat16)] + scratch
    args = [rows_view(source) for source in sources]
    args += [] if new_left else [left]
    args += [] if sources else [right]
    args += earlier
    bounds = (phase * columns + first, phase * columns + last, first)
    sums_size = (last - first) * SC * LANES * LANES * 4
    return pl.pallas_call(
        functools.partial(
            product_kernel, code_at, bounds, new_left, len(sources), len(earlier), keep
        ),
        in_specs=[smem] + [vmem] * len(args),
        out_specs=[vmem] * len(out_shape),
        out_shape=out_shape,
        scratch_shapes=scratch,
        compiler_params=pltpu.CompilerParams(vmem_limit_bytes=16 * MIB + 2 * sums_size),
        cost_estimate=pl.CostEstimate(flops=1_000_000, bytes_accessed=MIB, transcendentals=0),
    )(meta, *args)


def per_device(columns, rows, p_blocks, products):
    own_blocks = p_blocks[0]
    slots = own_blocks.shape[0]
    chips = rows // 2
    row, col = lax.axis_index("row"), lax.axis_index("col")
    swap = [(device, device ^ 1) for device in range(rows)]

    straight = []
    for hop in range(1, chips):
        jump = [((device + 2 * hop) % rows, device) for device in range(rows)]
        straight.append(lax.ppermute(own_blocks, "row", jump))
    sibling = lax.ppermute(own_blocks, "row", swap)

    meta, code_at = plan(products[0, 0], slots, row, col, columns, chips)
    made = functools.partial(products_of, meta, code_at, columns)
    everything = (0, columns)
    left, *parts = made(0, everything, [own_blocks, sibling], None, None, [])
    for hop, blocks in enumerate(straight):
        blocks, left, *parts = lax.optimization_barrier((blocks, left, *parts))
        crossed = lax.ppermute(blocks, "row", swap)
        parts = made(2 * hop + 1, everything, [blocks], left, None, parts)
        if hop + 1 < len(straight):
            parts = made(2 * hop + 2, everything, [crossed], left, None, parts)

    arrived = []
    begin, right = 0, None
    for turns in sent_order(columns):
        places = (begin, begin + len(turns))
        before = parts[places[0] : places[1]]
        phase = 2 * len(straight)
        if right is None:
            right, *sums = made(phase, places, [crossed], left, None, before, keep=True)
        else:
            sums = made(phase, places, [], left, right, before)
        for turn, part in zip(turns, sums):
            ahead = [(device, (device + turn) % columns) for device in range(columns)]
            arrived.append(lax.ppermute(part, "col", ahead) if turn else part)
        begin = places[1]

    vmem = pl.BlockSpec(memory_space=pltpu.VMEM)
    owned = pl.pallas_call(
        last_kernel,
        in_specs=[vmem] * columns,
        out_specs=vmem,
        out_shape=jax.ShapeDtypeStruct((SC * HALF, LANES), jnp.float32),
        scratch_shapes=[pltpu.VMEM((LANES, LANES), jnp.float32)],
        compiler_params=pltpu.CompilerParams(vmem_limit_bytes=16 * MIB),
    )(*arrived)
    return blocks_view(owned)[None]


def solution(mesh):
    columns, rows = mesh.shape["col"], mesh.shape["row"]
    return jax.shard_map(
        functools.partial(per_device, columns, rows),
        mesh=mesh,
        in_specs=(P(("groups", "col"), "row", None), P(("groups", "col"), "row", None, None)),
        out_specs=P(("groups", "row"), "col", None),
        check_vma=False,
    )
```

time: 74.2 us -> 55.9 us (0.75)
  the two profiles are of different devices: /device:TPU:11 before, /device:TPU:0 now
where the time goes in v2:
time: 55.9 us; the launch traced here: 56.9 us
  waiting for transfers between devices  18.4 us (33%)
  starting transfers between devices  15.4 us (28%)
  Pallas kernels  13 us (23%)
  other arithmetic  7.11 us (13%)
  local copies, waits for them, and re-layouts  2.87 us (5%)
    ppermute x3, starting transfers between devices, per_device(): arrived.append(lax.ppermute(part, 'col', ahead) if turn else part)  12.5 us
    pallas_call x5, Pallas kernels, products_of(): pl.pallas_call(functools.partial(product_kernel, code_at, bounds, new_lef...  12 us
    ppermute x3, waiting for transfers between devices, per_device(): arrived.append(lax.ppermute(part, 'col', ahead) if turn else part)  9.56 us
    ppermute x1, waiting for transfers between devices, per_device(): straight.append(lax.ppermute(own_blocks, 'row', jump))  8.47 us
    sort x1, other arithmetic, plan(): codes = lax.sort(segment << 13 | panel_slot << 6 | second)  5.04 us
    ppermute x1, starting transfers between devices, per_device(): straight.append(lax.ppermute(own_blocks, 'row', jump))  2.49 us
    unnamed x2, local copies, waits for them, and re-layouts  1.22 us
  transfers between devices with their start and end apart: 6, of which 5 were waited for; matrix products, arithmetic and copies ran while one was open for 15% of the time, Pallas kernels for 15%

profile of v2, /device:TPU:0, one launch (start us, length us, event | category | flops | bytes accessed | tf_op | source)
XLA Modules:
  0.0 56.9 jit_solution(4254921104312045029)
XLA Ops:
  0.0 0.5 collective-permute-start.1
  0.5 2.5 %collective-permute-start = (f32[64,4096]{1,0:T(8,128)}, f32[64,4096]{1,0:T(8,128)S(1)}, u32[]{:S(2)}, u32[]{:S(2)}) collective-permute-start(f32[64,4096]{1,0:T(8,128)} %bitcast.35), channel_id=1, source_target_pairs={{2,0},{3,1},{0,2},{1,3},{6,4},{7,5},{4,6},{5,7},{10,8},{11,9},{8,1... | collective-permute-start | bytes 3145736 | tf_op jit(solution)/shard_map/ppermute | solution.py:279
  2.9 0.7 %fusion.23 = (s32[1,1,1,2048]{3,1,2,0:T(1,128)S(1)}, s32[1,1,1,2048]{3,1,2,0:T(1,128)S(1)}, s32[1,1,1,2048]{3,1,2,0:T(1,128)S(1)}) fusion(s32[1,1,3,2048]{3,1,2,0:T(1,128)} %param.3), kind=kLoop, calls=%fused_computation.69 | loop fusion | bytes 49152 | tf_op jit(solution)/shard_map/slice | solution.py:183
  3.7 5.0 %sort.14 = (s32[2048]{0:T(1024)S(1)}, s32[2048]{0:T(1024)}) sort(s32[2048]{0:T(1024)S(1)} %fusion.11, s32[2048]{0:T(1024)S(1)} %iota.17), dimensions={0}, to_apply=%region_0.1 | sort | flops 22528 | bytes 32768 | tf_op jit(solution)/shard_map/sort | solution.py:199
  8.8 0.2 convert_reduce_fusion
  9.0 0.1 slice.51
  9.0 0.7 %fusion.24 = (s32[1]{0:T(128)}, s32[1]{0:T(128)}) fusion(s32[97]{0:T(128)S(1)} %convert_reduce_fusion), kind=kLoop, calls=%fused_computation.70 | loop fusion | bytes 16 | tf_op jit(solution)/shard_map/slice | solution.py:216
  9.7 0.8 %pad_add_fusion.1 = s32[97]{0:T(128)S(1)} fusion(s32[1]{0:T(128)} %get-tuple-element.53, s32[96]{0:T(128)S(1)} %slice.51), kind=kLoop, calls=%fused_computation.65 | loop fusion | flops 97 | bytes 776 | tf_op jit(solution)/shard_map/concatenate | solution.py:215
  10.5 0.1 slice_subtract_fusion
  10.5 0.1 select_reduce_fusion.2
  10.7 0.1 slice.55
  10.7 0.1 slice.53
  10.8 0.1 slice_subtract_fusion.1
  10.9 0.1 convert_reduce_fusion.1
  11.1 0.7 %fusion.22 = s32[640]{0:T(1024)S(1)} fusion(s32[640]{0:T(1024)S(1)} %get-tuple-element.47, s32[640]{0:T(1024)S(1)} %get-tuple-element.48, s32[640]{0:T(1024)S(1)} %get-tuple-element.46, s32[]{:T(128)} %bitcast.4, s32[]{:T(128)S(1)} %bitcast.42), kind=kLoop, calls=%fused_computation.59 | loop fusion | flops 14080 | bytes 10248 | tf_op jit(solution)/shard_map/or | solution.py:219
  11.8 0.0 collective-permute-done.1
  11.8 0.0 copy-start
  11.8 1.2 %copy-done = f32[1,64,4096]{2,1,0:T(8,128)S(1)} copy-done((f32[1,64,4096]{2,1,0:T(8,128)S(1)}, f32[1,64,4096]{2,1,0:T(8,128)}, u32[]{:S(2)}) %copy-start) | copy-done | bytes 1048600
  13.0 5.5 %shard_map.28 = (bf16[8320,128]{1,0:T(8,128)(2,1)S(1)}, f32[4,64,128]{2,1,0:T(8,128)S(1)}, f32[4,64,128]{2,1,0:T(8,128)S(1)}, f32[4,64,128]{2,1,0:T(8,128)S(1)}, f32[4,64,128]{2,1,0:T(8,128)S(1)}) custom-call(s32[3072]{0:T(1024)S(1)} %fusion.1.refs_0_, f32[2048,128]{1,0:T(8,128)S(1)} %bitcast.36, f32[2048,128]{1,0:T(8,128)S(1)} %bitcast.37), custom_call_target="tpu_custom_call" | custom-call | flops 1000000 | bytes 1048576 | tf_op jit(solution)/shard_map/pallas_call | solution.py:256
  18.5 8.5 %collective-permute-done = f32[64,4096]{1,0:T(8,128)S(1)} collective-permute-done((f32[64,4096]{1,0:T(8,128)}, f32[64,4096]{1,0:T(8,128)S(1)}, u32[]{:S(2)}, u32[]{:S(2)}) %collective-permute-start) | collective-permute-done | bytes 1048608 | tf_op jit(solution)/shard_map/ppermute | solution.py:279
  27.0 0.0 collective-permute-start.2
  27.0 2.2 %shard_map.29 = (f32[4,64,128]{2,1,0:T(8,128)S(1)}, f32[4,64,128]{2,1,0:T(8,128)S(1)}, f32[4,64,128]{2,1,0:T(8,128)S(1)}, f32[4,64,128]{2,1,0:T(8,128)S(1)}) custom-call(s32[3072]{0:T(1024)S(1)} %fusion.1.refs_0_, f32[2048,128]{1,0:T(8,128)S(1)} %bitcast.33, bf16[8320,128]{1,0:T(8,128)(2,1)S(1)} %get-tuple-element.33.refs_2_.refs_1_, ...), custom_call_target="tpu_custom_call" | custom-call | flops 1000000 | bytes 1048576 | tf_op jit(solution)/shard_map/pallas_call | solution.py:256
  29.2 0.4 collective-permute-done.2
  29.6 1.9 %shard_map.30 = (bf16[2048,256]{1,0:T(8,128)(2,1)S(1)}, f32[4,64,128]{2,1,0:T(8,128)S(1)}) custom-call(s32[3072]{0:T(1024)S(1)} %fusion.1.refs_0_, f32[2048,128]{1,0:T(8,128)S(1)} %bitcast.38, bf16[8320,128]{1,0:T(8,128)(2,1)S(1)} %get-tuple-element.33.refs_2_.refs_1_, f32[4,64,128]{2,1,0:T(8,128)S(1)} %get-tuple-element.38.refs_3_), custom_call_target="tpu_custom_call" | custom-call | flops 1000000 | bytes 1048576 | tf_op jit(solution)/shard_map/pallas_call | solution.py:256
  31.6 1.4 %shard_map.31 = (f32[4,64,128]{2,1,0:T(8,128)S(1)}, f32[4,64,128]{2,1,0:T(8,128)S(1)}) custom-call(s32[3072]{0:T(1024)S(1)} %fusion.1.refs_0_, bf16[8320,128]{1,0:T(8,128)(2,1)S(1)} %get-tuple-element.33.refs_2_.refs_1_, bf16[2048,256]{1,0:T(8,128)(2,1)S(1)} %get-tuple-element.40.refs_2_, f32[4,64,128]{2,1,0:T(8,128)S(1)} %get-tuple-element.41.refs_3_, ...), custom_call_target="tpu_custom_call" | custom-call | flops 1000000 | bytes 1048576 | tf_op jit(solution)/shard_map/pallas_call | solution.py:256
  33.0 8.8 %collective-permute-start.4 = (f32[4,64,128]{2,1,0:T(8,128)S(1)}, f32[4,64,128]{2,1,0:T(8,128)S(1)}, u32[]{:S(2)}, u32[]{:S(2)}) collective-permute-start(f32[4,64,128]{2,1,0:T(8,128)S(1)} %get-tuple-element.43), channel_id=1, source_target_pairs={{0,4},{4,8},{8,12},{12,0},{1,5},{5,9},{9,13},{13,1},{2,6},{6,10},{... | collective-permute-start | bytes 393224 | tf_op jit(solution)/shard_map/ppermute | solution.py:305
  41.8 1.5 %collective-permute-start.5 = (f32[4,64,128]{2,1,0:T(8,128)S(1)}, f32[4,64,128]{2,1,0:T(8,128)S(1)}, u32[]{:S(2)}, u32[]{:S(2)}) collective-permute-start(f32[4,64,128]{2,1,0:T(8,128)S(1)} %get-tuple-element.44), channel_id=1, source_target_pairs={{0,12},{4,0},{8,4},{12,8},{1,13},{5,1},{9,5},{13,9},{2,14},{6,2},{... | collective-permute-start | bytes 393224 | tf_op jit(solution)/shard_map/ppermute | solution.py:305
  43.3 2.2 %collective-permute-start.3 = (f32[4,64,128]{2,1,0:T(8,128)S(1)}, f32[4,64,128]{2,1,0:T(8,128)S(1)}, u32[]{:S(2)}, u32[]{:S(2)}) collective-permute-start(f32[4,64,128]{2,1,0:T(8,128)S(1)} %get-tuple-element.39), channel_id=1, source_target_pairs={{0,8},{4,12},{8,0},{12,4},{1,9},{5,13},{9,1},{13,5},{2,10},{6,14},... | collective-permute-start | bytes 393224 | tf_op jit(solution)/shard_map/ppermute | solution.py:305
  45.5 0.9 %shard_map.32.refs_3_ = f32[4,64,128]{2,1,0:T(8,128)S(1)} custom-call(s32[3072]{0:T(1024)S(1)} %fusion.1.refs_0_, bf16[8320,128]{1,0:T(8,128)(2,1)S(1)} %get-tuple-element.33.refs_2_.refs_1_, bf16[2048,256]{1,0:T(8,128)(2,1)S(1)} %get-tuple-element.40.refs_2_, f32[4,64,128]{2,1,0:T(8,128)S(1)} %get-tuple-element.45.refs_3_), custom_call_target="tpu_custom_call" | custom-call | flops 1000000 | bytes 1048576 | tf_op jit(solution)/shard_map/pallas_call | solution.py:256
  46.4 1.3 %collective-permute-done.4.refs_1_ = f32[4,64,128]{2,1,0:T(8,128)S(1)} collective-permute-done((f32[4,64,128]{2,1,0:T(8,128)S(1)}, f32[4,64,128]{2,1,0:T(8,128)S(1)}, u32[]{:S(2)}, u32[]{:S(2)}) %collective-permute-start.4) | collective-permute-done | bytes 131104 | tf_op jit(solution)/shard_map/ppermute | solution.py:305
  47.7 1.5 %collective-permute-done.5.refs_2_ = f32[4,64,128]{2,1,0:T(8,128)S(1)} collective-permute-done((f32[4,64,128]{2,1,0:T(8,128)S(1)}, f32[4,64,128]{2,1,0:T(8,128)S(1)}, u32[]{:S(2)}, u32[]{:S(2)}) %collective-permute-start.5) | collective-permute-done | bytes 131104 | tf_op jit(solution)/shard_map/ppermute | solution.py:305
  49.2 6.8 %collective-permute-done.3.refs_0_ = f32[4,64,128]{2,1,0:T(8,128)S(1)} collective-permute-done((f32[4,64,128]{2,1,0:T(8,128)S(1)}, f32[4,64,128]{2,1,0:T(8,128)S(1)}, u32[]{:S(2)}, u32[]{:S(2)}) %collective-permute-start.3) | collective-permute-done | bytes 131104 | tf_op jit(solution)/shard_map/ppermute | solution.py:305
  56.0 0.9 %shard_map.33 = f32[256,128]{1,0:T(8,128)} custom-call(f32[4,64,128]{2,1,0:T(8,128)S(1)} %collective-permute-done.3.refs_0_, f32[4,64,128]{2,1,0:T(8,128)S(1)} %collective-permute-done.4.refs_1_, f32[4,64,128]{2,1,0:T(8,128)S(1)} %collective-permute-done.5.refs_2_, f32[4,64,128]{2,1,0:T(8,128)S(1)} %shard_map.32.refs_3_), custom_call_target="tpu_custom_call" | custom-call | tf_op jit(solution)/shard_map/pallas_call | solution.py:309
  (7 shorter events, 0.1 us)
Async XLA Ops:
  0.0 11.8 %collective-permute-start.1 = (f32[64,4096]{1,0:T(8,128)}, f32[64,4096]{1,0:T(8,128)S(1)}, u32[]{:S(2)}, u32[]{:S(2)}) collective-permute-start(f32[64,4096]{1,0:T(8,128)} %bitcast.34), channel_id=1, source_target_pairs={{0,1},{1,0},{2,3},{3,2},{4,5},{5,4},{6,7},{7,6},{8,9},{9,8},{10,11... | collective-permute-start | bytes 3145736 | tf_op jit(solution)/shard_map/ppermute | solution.py:280
  0.5 26.5 %collective-permute-start = (f32[64,4096]{1,0:T(8,128)}, f32[64,4096]{1,0:T(8,128)S(1)}, u32[]{:S(2)}, u32[]{:S(2)}) collective-permute-start(f32[64,4096]{1,0:T(8,128)} %bitcast.35), channel_id=1, source_target_pairs={{2,0},{3,1},{0,2},{1,3},{6,4},{7,5},{4,6},{5,7},{10,8},{11,9},{8,1... | collective-permute-start | bytes 3145736 | tf_op jit(solution)/shard_map/ppermute | solution.py:279
  11.8 1.2 %copy-start = (f32[1,64,4096]{2,1,0:T(8,128)S(1)}, f32[1,64,4096]{2,1,0:T(8,128)}, u32[]{:S(2)}) copy-start(f32[1,64,4096]{2,1,0:T(8,128)} %param.2) | copy-start | bytes 3145732
  27.0 2.7 %collective-permute-start.2 = (f32[64,4096]{1,0:T(8,128)S(1)}, f32[64,4096]{1,0:T(8,128)S(1)}, u32[]{:S(2)}, u32[]{:S(2)}) collective-permute-start(f32[64,4096]{1,0:T(8,128)S(1)} %collective-permute-done), channel_id=1, source_target_pairs={{0,1},{1,0},{2,3},{3,2},{4,5},{5,4},{6,7},{7,6},{8,9},{9,8},{10,11... | collective-permute-start | bytes 3145736 | tf_op jit(solution)/shard_map/ppermute | solution.py:288
  33.0 14.7 %collective-permute-start.4 = (f32[4,64,128]{2,1,0:T(8,128)S(1)}, f32[4,64,128]{2,1,0:T(8,128)S(1)}, u32[]{:S(2)}, u32[]{:S(2)}) collective-permute-start(f32[4,64,128]{2,1,0:T(8,128)S(1)} %get-tuple-element.43), channel_id=1, source_target_pairs={{0,4},{4,8},{8,12},{12,0},{1,5},{5,9},{9,13},{13,1},{2,6},{6,10},{... | collective-permute-start | bytes 393224 | tf_op jit(solution)/shard_map/ppermute | solution.py:305
  41.8 7.4 %collective-permute-start.5 = (f32[4,64,128]{2,1,0:T(8,128)S(1)}, f32[4,64,128]{2,1,0:T(8,128)S(1)}, u32[]{:S(2)}, u32[]{:S(2)}) collective-permute-start(f32[4,64,128]{2,1,0:T(8,128)S(1)} %get-tuple-element.44), channel_id=1, source_target_pairs={{0,12},{4,0},{8,4},{12,8},{1,13},{5,1},{9,5},{13,9},{2,14},{6,2},{... | collective-permute-start | bytes 393224 | tf_op jit(solution)/shard_map/ppermute | solution.py:305
  43.3 12.7 %collective-permute-start.3 = (f32[4,64,128]{2,1,0:T(8,128)S(1)}, f32[4,64,128]{2,1,0:T(8,128)S(1)}, u32[]{:S(2)}, u32[]{:S(2)}) collective-permute-start(f32[4,64,128]{2,1,0:T(8,128)S(1)} %get-tuple-element.39), channel_id=1, source_target_pairs={{0,8},{4,12},{8,0},{12,4},{1,9},{5,13},{9,1},{13,5},{2,10},{6,14},... | collective-permute-start | bytes 393224 | tf_op jit(solution)/shard_map/ppermute | solution.py:305

commit v3 on v2

v3 whole, which is shorter than its diff:
```python
import functools

import jax
import jax.numpy as jnp
from jax import lax
from jax.experimental import pallas as pl
from jax.experimental.pallas import tpu as pltpu
from jax.sharding import PartitionSpec as P

BLK = 64
BB = 4096
SC = 8
HALF = 32
LANES = 128
GROUP = 4
UNROLLS = (32, 8)
MIB = 1 << 20


def rows_view(blocks):
    count = blocks.shape[0]
    tiles = blocks.reshape(count // 8, 8, HALF, LANES)
    return tiles.transpose(0, 2, 1, 3).reshape(count * HALF, LANES)


def blocks_view(rows):
    count = rows.shape[0] // HALF
    tiles = rows.reshape(count // 8, HALF, 8, LANES)
    return tiles.transpose(0, 2, 1, 3).reshape(count, BB)


def block_rows(ref, slot):
    start = (slot // 8) * (8 * HALF) + slot % 8
    return ref[pl.ds(start, HALF, stride=8), :]


def high_low(rows):
    high = rows.astype(jnp.bfloat16)
    low = (rows - high.astype(jnp.float32)).astype(jnp.bfloat16)
    return high, low


def fill_right(source, right, first_block, count):
    def one(slot, carry):
        high, low = high_low(block_rows(source, slot))
        at = pl.ds(pl.multiple_of((first_block + slot) * HALF, HALF), HALF)
        right[at, :LANES] = high
        right[at, LANES:] = low
        return carry

    lax.fori_loop(0, count, one, 0, unroll=8)


def fill_left(source, left, count):
    near = lax.broadcasted_iota(jnp.int32, (LANES, LANES), 1) < BLK

    def two(number, carry):
        pair = high_low(block_rows(source, 2 * number)) + high_low(block_rows(source, 2 * number + 1))
        straight = jnp.concatenate(pair, axis=0).T
        turned = pltpu.roll(straight, BLK, 1)
        at = pl.multiple_of(2 * number * LANES, LANES)
        left[pl.ds(at, LANES), :] = jnp.where(near, straight, turned)
        left[pl.ds(at + LANES, LANES), :] = jnp.where(near, turned, straight)
        return carry

    lax.fori_loop(0, count // 2, two, 0, unroll=4)
    left[pl.ds(count * LANES, LANES), :] = jnp.zeros((LANES, LANES), jnp.bfloat16)


def run_groups(meta, layout, bounds, empty, left, right, sums):
    groups_at, code_at = layout
    begin, end = meta[bounds[0]], meta[bounds[1]]
    first_target = bounds[2] * SC
    near = lax.broadcasted_iota(jnp.int32, (LANES, LANES), 1) < BLK

    def multiply(place):
        group = meta[groups_at + place]
        base = group >> 12
        live = jnp.where(place < end, (group >> 8) & 15, 0)
        target = jnp.clip((group & 255) - first_target, 0, sums.shape[0] // LANES - 1)
        lefts, rights = [], []
        for item in range(GROUP):
            code = meta[code_at + base + item]
            own = jnp.where(item < live, code & 63, empty)
            other = jnp.where(item < live, (code >> 6) & 127, 0)
            lefts.append(left[pl.ds(pl.multiple_of(own * LANES, LANES), LANES), :])
            block = right[pl.ds(pl.multiple_of(other * HALF, HALF), HALF), :]
            rights += [block, block]
        stacked = jnp.concatenate(
            [jnp.where(near, lefts[item], lefts[item + 1]) for item in range(0, GROUP, 2)],
            axis=1,
        )
        term = jnp.dot(
            stacked, jnp.concatenate(rights, axis=0), preferred_element_type=jnp.float32
        )
        at = pl.ds(pl.multiple_of(target * LANES, LANES), LANES)
        sums[at, :] += term[:, :LANES] + term[:, LANES:]

    wide, narrow = UNROLLS

    def wide_step(number, carry):
        for inner in range(wide):
            multiply(begin + number * wide + inner)
        return carry

    whole = (end - begin) // wide
    middle = begin + whole * wide

    def narrow_step(number, carry):
        for inner in range(narrow):
            multiply(middle + number * narrow + inner)
        return carry

    lax.fori_loop(0, whole, wide_step, 0)
    lax.fori_loop(0, (end - middle + narrow - 1) // narrow, narrow_step, 0)


def clear(sums):
    def one(number, carry):
        at = pl.ds(pl.multiple_of(number * LANES, LANES), LANES)
        sums[at, :] = jnp.zeros((LANES, LANES), jnp.float32)
        return carry

    lax.fori_loop(0, sums.shape[0] // LANES, one, 0, unroll=2)


def pack_pairs(sums, earlier, outs):
    near = lax.broadcasted_iota(jnp.int32, (BLK, LANES), 1) < BLK
    for place, out in enumerate(outs):
        for pair in range(SC // 2):
            at = (place * SC + 2 * pair) * LANES
            upper0 = sums[at : at + BLK, :]
            lower0 = sums[at + BLK : at + LANES, :]
            upper1 = sums[at + LANES : at + LANES + BLK, :]
            lower1 = sums[at + LANES + BLK : at + 2 * LANES, :]
            turned = pltpu.roll(jnp.where(near, upper1, lower0), BLK, 1)
            both = jnp.where(near, upper0, lower1) + turned
            for part in earlier[place :: len(outs)]:
                both = both + part[pair]
            out[pair] = both


def product_kernel(layout, bounds, new_left, rights, keep, earlier, meta, left, *refs):
    refs, sums = list(refs[:-1]), refs[-1]
    sources, earlier, refs = refs[:rights], refs[rights : rights + earlier], refs[rights + earlier :]
    if new_left:
        source, left = left, refs.pop(0)
        fill_left(source, left, source.shape[0] // HALF)
    if any(source.dtype == jnp.float32 for source in sources):
        right, at = refs.pop(0) if keep else refs.pop(), 0
        for source in sources:
            rows = source.shape[0]
            if source.dtype == jnp.float32:
                fill_right(source, right, at // HALF, rows // HALF)
            else:
                right[at : at + rows, :] = source[...]
            at += rows
    else:
        (right,) = sources
    clear(sums)
    run_groups(meta, layout, bounds, left.shape[0] // LANES - 1, left, right, sums)
    pack_pairs(sums, earlier, refs)


def last_kernel(*refs):
    parts, out, turned = refs[:-2], refs[-2], refs[-1]
    for pair in range(SC // 2):
        total = parts[0][pair]
        for part in parts[1:]:
            total = total + part[pair]
        turned[:, :BLK] = total.T
        even = turned[pl.ds(0, BLK, stride=2), :]
        odd = turned[pl.ds(1, BLK, stride=2), :]
        near = lax.broadcasted_iota(jnp.int32, (BLK, LANES), 1) < BLK
        packed = jnp.where(near, even, pltpu.roll(odd, BLK, 1))
        out[pl.ds(2 * pair, HALF, stride=8), :] = packed[:HALF]
        out[pl.ds(2 * pair + 1, HALF, stride=8), :] = packed[HALF:]


def sent_order(columns):
    half = columns // 2
    cut = half + half // 2
    groups = [range(half, cut), range(cut, columns), range(1, half), range(1)]
    return [list(pairs) for pairs in groups if len(pairs)]


def plan(lists, slots, row, col, columns, chips):
    first, second, target = lists[0], lists[1], lists[2]
    entries = first.shape[0]
    targets = columns * SC
    phases = chips + 1
    shard, slot = first // slots, first % slots
    hop = (shard // 2 - row // 2) % chips
    crossed = (shard ^ row) & 1
    pair = (target // SC) ^ col
    half = columns // 2
    position = jnp.where(pair >= half, pair - half, jnp.where(pair == 0, columns, pair + half) - 1)
    apart = (hop == chips - 1) & (position < len(sent_order(columns)[0]))
    phase = hop + jnp.where(apart, crossed, 0)
    slot = crossed * slots + slot
    segments = phases * targets
    segment = jnp.where(target < targets, phase * targets + position * SC + target % SC, segments)
    (codes,) = lax.sort(((segment << 13) | (slot << 6) | second,), is_stable=False)

    count = lambda chosen, amount: jnp.sum(jnp.where(chosen, amount, 0), axis=1)
    edges = jnp.arange(segments)
    live = count((codes >> 13)[None, :] == edges[:, None], 1)
    groups = (live + GROUP - 1) // GROUP
    stops = count(edges[None, :] <= edges[:, None], groups[None, :])
    places = -(-(entries // GROUP + segments + UNROLLS[0]) // LANES) * LANES
    place = jnp.arange(places)[:, None]
    passed = stops[None, :] <= place
    in_segment = count(passed, 1)
    base = GROUP * place[:, 0] + count(passed, (live - GROUP * groups)[None, :])
    base = jnp.clip(base, 0, entries)
    stop = count((stops - groups)[None, :] <= place, live[None, :])
    valid = jnp.clip(stop - base, 0, GROUP)
    described = (base << 12) | (valid << 8) | (in_segment % targets)

    head = -(-(segments // SC + 1) // LANES) * LANES
    bounds = count(edges[None, :] < SC * jnp.arange(head)[:, None], groups[None, :])
    meta = jnp.concatenate([bounds, described, codes, jnp.zeros((LANES,), jnp.int32)])
    return meta, (head, head + places)


def products_of(columns, meta, layout, phase, places, left, rights, earlier, keep=False):
    smem = pl.BlockSpec(memory_space=pltpu.SMEM)
    vmem = pl.BlockSpec(memory_space=pltpu.VMEM)
    part = jax.ShapeDtypeStruct((SC // 2, BLK, LANES), jnp.float32)
    first, last = places
    targets = (last - first) * SC
    out_shape, scratch = [], [pltpu.VMEM((targets * LANES, LANES), jnp.float32)]
    new_left = left.dtype == jnp.float32
    if new_left:
        out_shape.append(jax.ShapeDtypeStruct(((left.shape[0] + 1) * LANES, LANES), jnp.bfloat16))
        left = rows_view(left)
    new_right = any(right.dtype == jnp.float32 for right in rights)
    rights = [rows_view(right) if right.dtype == jnp.float32 else right for right in rights]
    if new_right:
        table = (sum(right.shape[0] for right in rights), 2 * LANES)
        if keep:
            out_shape.append(jax.ShapeDtypeStruct(table, jnp.bfloat16))
        else:
            scratch.insert(0, pltpu.VMEM(table, jnp.bfloat16))
    out_shape += [part] * (last - first)
    bounds = (phase * columns + first, phase * columns + last, first)
    args = [left, *rights, *earlier]
    return pl.pallas_call(
        functools.partial(
            product_kernel, layout, bounds, new_left, len(rights), keep, len(earlier)
        ),
        in_specs=[smem] + [vmem] * len(args),
        out_specs=[vmem] * len(out_shape),
        out_shape=out_shape,
        scratch_shapes=scratch,
        compiler_params=pltpu.CompilerParams(
            vmem_limit_bytes=16 * MIB + 8 * targets * LANES * LANES
        ),
        cost_estimate=pl.CostEstimate(flops=1_000_000, bytes_accessed=MIB, transcendentals=0),
    )(meta, *args)


def per_device(columns, rows, p_blocks, products):
    own_blocks = p_blocks[0]
    slots = own_blocks.shape[0]
    chips = rows // 2
    row, col = lax.axis_index("row"), lax.axis_index("col")
    swap = [(device, device ^ 1) for device in range(rows)]

    arriving = []
    for hop in range(1, chips):
        jump = [((device + 2 * hop) % rows, device) for device in range(rows)]
        arriving.append(lax.ppermute(own_blocks, "row", jump))
    sibling_blocks = lax.ppermute(own_blocks, "row", swap)

    made = functools.partial(
        products_of, columns, *plan(products[0, 0], slots, row, col, columns, chips)
    )
    whole = (0, columns)
    left, *parts = made(0, whole, own_blocks, [own_blocks, sibling_blocks], [])
    for hop, blocks in enumerate(arriving[:-1], 1):
        blocks, left, *parts = lax.optimization_barrier((blocks, left, *parts))
        parts = made(hop, whole, left, [blocks, lax.ppermute(blocks, "row", swap)], parts)
    blocks, left, *parts = lax.optimization_barrier((arriving[-1], left, *parts))
    crossed = lax.ppermute(blocks, "row", swap)

    arrived, early, begin = [], [], 0
    for number, pairs in enumerate(sent_order(columns)):
        end = begin + len(pairs)
        places, earlier = (begin, end), parts[begin:end]
        if number == 0:
            right, *earlier = made(chips - 1, places, left, [blocks], earlier, keep=True)
            right, *sums = made(chips, places, left, [right, crossed], earlier, keep=True)
        else:
            if pairs == [0]:
                earlier = [*earlier, *early]
            sums = made(chips - 1, places, left, [right], earlier)
        for pair, part in zip(pairs, sums):
            across = [(device, device ^ pair) for device in range(columns)]
            moved = lax.ppermute(part, "col", across) if pair else part
            (arrived if number else early).append(moved)
        begin = end

    vmem = pl.BlockSpec(memory_space=pltpu.VMEM)
    owned = pl.pallas_call(
        last_kernel,
        in_specs=[vmem] * len(arrived),
        out_specs=vmem,
        out_shape=jax.ShapeDtypeStruct((SC * HALF, LANES), jnp.float32),
        scratch_shapes=[pltpu.VMEM((LANES, LANES), jnp.float32)],
        compiler_params=pltpu.CompilerParams(vmem_limit_bytes=16 * MIB),
    )(*arrived)
    return blocks_view(owned)[None]


def solution(mesh):
    columns, rows = mesh.shape["col"], mesh.shape["row"]
    return jax.shard_map(
        functools.partial(per_device, columns, rows),
        mesh=mesh,
        in_specs=(P(("groups", "col"), "row", None), P(("groups", "col"), "row", None, None)),
        out_specs=P(("groups", "row"), "col", None),
        check_vma=False,
    )
```

time: 55.9 us -> 50.5 us (0.903); the launches traced: 56.9 us -> 50.9 us
  Pallas kernels: 13 us -> 27.9 us
  starting transfers between devices: 15.4 us -> 4.93 us
  waiting for transfers between devices: 18.4 us -> 11.2 us
  other arithmetic: 7.11 us -> 4.9 us
  local copies, waits for them, and re-layouts: 2.87 us -> 1.95 us
    pallas_call x6 -> x7, Pallas kernels: 13 us -> 27.9 us  [the longest x6 26.9 us: products_of(): pl.pallas_call(functools.partial(product_kernel, layout, bounds, new_left...]
    ppermute x5, starting transfers between devices: 15.4 us -> 4.93 us  [the longest x1 2.49 us: per_device(): arriving.append(lax.ppermute(own_blocks, 'row', jump))]
    ppermute x5, waiting for transfers between devices: 18 us -> 11.2 us  [the longest x1 5.87 us: per_device(): arriving.append(lax.ppermute(own_blocks, 'row', jump))]
    slice x4 -> x0, local copies, waits for them, and re-layouts: 0.91 us -> none  [the longest x1 0.67 us: plan(): stops[0]]
    sort x1, other arithmetic: 5.04 us -> 4.26 us  [plan(): codes, = lax.sort((segment << 13 | slot << 6 | second,), is_stable=False)]
    concatenate x2 -> x1, other arithmetic: 0.77 us -> 0.01 us  [plan(): jnp.concatenate([bounds, described, codes, jnp.zeros((LANES,), jnp.int32)])]
    or x1, other arithmetic: 0.66 us -> 0.01 us  [plan(): described = base << 12 | valid << 8 | in_segment % targets]
  transfers between devices with their start and end apart: 6 -> 6, of which waited for: 5 -> 4; matrix products, arithmetic and copies ran while one was open for 15% -> 11% of each run, Pallas kernels for 15% -> 47%
where the time goes in v3:
time: 50.5 us; the launch traced here: 50.9 us
  Pallas kernels  27.9 us (55%)
  waiting for transfers between devices  11.2 us (22%)
  starting transfers between devices  4.93 us (10%)
  other arithmetic  4.9 us (10%)
  local copies, waits for them, and re-layouts  1.95 us (4%)
    pallas_call x6, Pallas kernels, products_of(): pl.pallas_call(functools.partial(product_kernel, layout, bounds, new_left...  26.9 us
    ppermute x1, waiting for transfers between devices, per_device(): arriving.append(lax.ppermute(own_blocks, 'row', jump))  5.87 us
    ppermute x3, waiting for transfers between devices, per_device(): moved = lax.ppermute(part, 'col', across) if pair else part  5.29 us
    sort x1, other arithmetic, plan(): codes, = lax.sort((segment << 13 | slot << 6 | second,), is_stable=False)  4.26 us
    ppermute x1, starting transfers between devices, per_device(): arriving.append(lax.ppermute(own_blocks, 'row', jump))  2.49 us
    ppermute x3, starting transfers between devices, per_device(): moved = lax.ppermute(part, 'col', across) if pair else part  1.99 us
    unnamed x2, local copies, waits for them, and re-layouts  1.22 us
  transfers between devices with their start and end apart: 6, of which 4 were waited for; matrix products, arithmetic and copies ran while one was open for 11% of the time, Pallas kernels for 47%

profile of v3, /device:TPU:0, one launch (start us, length us, event | category | flops | bytes accessed | tf_op | source)
XLA Modules:
  0.0 50.9 jit_solution(17217314685350841709)
XLA Ops:
  0.0 0.5 collective-permute-start.1
  0.5 2.5 %collective-permute-start = (f32[64,4096]{1,0:T(8,128)}, f32[64,4096]{1,0:T(8,128)S(1)}, u32[]{:S(2)}, u32[]{:S(2)}) collective-permute-start(f32[64,4096]{1,0:T(8,128)} %bitcast.30), channel_id=1, source_target_pairs={{2,0},{3,1},{0,2},{1,3},{6,4},{7,5},{4,6},{5,7},{10,8},{11,9},{8,1... | collective-permute-start | bytes 3145736 | tf_op jit(solution)/shard_map/ppermute | solution.py:273
  2.9 0.7 %fusion.16 = (s32[1,1,1,2048]{3,1,2,0:T(1,128)S(1)}, s32[1,1,1,2048]{3,1,2,0:T(1,128)S(1)}, s32[1,1,1,2048]{3,1,2,0:T(1,128)S(1)}) fusion(s32[1,1,3,2048]{3,1,2,0:T(1,128)} %param.3), kind=kLoop, calls=%fused_computation.59 | loop fusion | bytes 49152 | tf_op jit(solution)/shard_map/slice | solution.py:188
  3.7 4.3 %sort.7 = s32[2048]{0:T(1024)S(1)} sort(s32[2048]{0:T(1024)S(1)} %fusion.8), dimensions={0}, to_apply=%region_0.1 | sort | flops 22528 | bytes 16384 | tf_op jit(solution)/shard_map/sort | solution.py:203
  8.0 0.2 select_reduce_fusion
  8.2 0.1 select_reduce_fusion.4
  8.3 0.1 select_reduce_fusion.5
  8.4 0.1 select_reduce_fusion.1
  8.6 0.0 collective-permute-done.1
  8.6 0.0 copy-start
  8.7 1.2 %copy-done = f32[1,64,4096]{2,1,0:T(8,128)S(1)} copy-done((f32[1,64,4096]{2,1,0:T(8,128)S(1)}, f32[1,64,4096]{2,1,0:T(8,128)}, u32[]{:S(2)}) %copy-start) | copy-done | bytes 1048600
  9.9 11.2 %shard_map.28 = (bf16[8320,128]{1,0:T(8,128)(2,1)S(1)}, f32[4,64,128]{2,1,0:T(8,128)S(1)}, f32[4,64,128]{2,1,0:T(8,128)S(1)}, f32[4,64,128]{2,1,0:T(8,128)S(1)}, f32[4,64,128]{2,1,0:T(8,128)S(1)}) custom-call(s32[2944]{0:T(1024)S(1)} %pad_add_fusion.meta, f32[2048,128]{1,0:T(8,128)S(1)} %bitcast.31, f32[2048,128]{1,0:T(8,128)S(1)} %bitcast.32, ...), custom_call_target="tpu_custom_call" | custom-call | flops 1000000 | bytes 1048576 | tf_op jit(solution)/shard_map/pallas_call | solution.py:248
  21.1 5.9 %collective-permute-done = f32[64,4096]{1,0:T(8,128)S(1)} collective-permute-done((f32[64,4096]{1,0:T(8,128)}, f32[64,4096]{1,0:T(8,128)S(1)}, u32[]{:S(2)}, u32[]{:S(2)}) %collective-permute-start) | collective-permute-done | bytes 1048608 | tf_op jit(solution)/shard_map/ppermute | solution.py:273
  27.0 0.0 collective-permute-start.2
  27.0 3.0 %shard_map.29 = (bf16[2048,256]{1,0:T(8,128)(2,1)S(1)}, f32[4,64,128]{2,1,0:T(8,128)S(1)}) custom-call(s32[2944]{0:T(1024)S(1)} %pad_add_fusion.meta, bf16[8320,128]{1,0:T(8,128)(2,1)S(1)} %get-tuple-element.25.left, f32[2048,128]{1,0:T(8,128)S(1)} %bitcast.34, f32[4,64,128]{2,1,0:T(8,128)S(1)} %get-tuple-element.27.refs_1_), custom_call_target="tpu_custom_call" | custom-call | flops 1000000 | bytes 1048576 | tf_op jit(solution)/shard_map/pallas_call | solution.py:248
  30.0 0.0 collective-permute-done.2
  30.0 3.0 %shard_map.30 = (bf16[4096,256]{1,0:T(8,128)(2,1)S(1)}, f32[4,64,128]{2,1,0:T(8,128)S(1)}) custom-call(s32[2944]{0:T(1024)S(1)} %pad_add_fusion.meta, bf16[8320,128]{1,0:T(8,128)(2,1)S(1)} %get-tuple-element.25.left, bf16[2048,256]{1,0:T(8,128)(2,1)S(1)} %get-tuple-element.28.refs_0_, f32[2048,128]{1,0:T(8,128)S(1)} %bitcast.33, ...), custom_call_target="tpu_custom_call" | custom-call | flops 1000000 | bytes 1048576 | tf_op jit(solution)/shard_map/pallas_call | solution.py:248
  33.0 1.8 %collective-permute-start.5 = (f32[4,64,128]{2,1,0:T(8,128)S(1)}, f32[4,64,128]{2,1,0:T(8,128)S(1)}, u32[]{:S(2)}, u32[]{:S(2)}) collective-permute-start(f32[4,64,128]{2,1,0:T(8,128)S(1)} %get-tuple-element.34), channel_id=1, source_target_pairs={{0,8},{4,12},{8,0},{12,4},{1,9},{5,13},{9,1},{13,5},{2,10},{6,14},... | collective-permute-start | bytes 393224 | tf_op jit(solution)/shard_map/ppermute | solution.py:300
  34.9 3.0 %shard_map.32 = f32[4,64,128]{2,1,0:T(8,128)S(1)} custom-call(s32[2944]{0:T(1024)S(1)} %pad_add_fusion.meta, bf16[8320,128]{1,0:T(8,128)(2,1)S(1)} %get-tuple-element.25.left, bf16[4096,256]{1,0:T(8,128)(2,1)S(1)} %get-tuple-element.30.refs_0_, f32[4,64,128]{2,1,0:T(8,128)S(1)} %get-tuple-element.32.refs_1_), custom_call_target="tpu_custom_call" | custom-call | flops 1000000 | bytes 1048576 | tf_op jit(solution)/shard_map/pallas_call | solution.py:248
  37.8 3.3 %shard_map.31 = f32[4,64,128]{2,1,0:T(8,128)S(1)} custom-call(s32[2944]{0:T(1024)S(1)} %pad_add_fusion.meta, bf16[8320,128]{1,0:T(8,128)(2,1)S(1)} %get-tuple-element.25.left, bf16[4096,256]{1,0:T(8,128)(2,1)S(1)} %get-tuple-element.30.refs_0_, f32[4,64,128]{2,1,0:T(8,128)S(1)} %get-tuple-element.31.refs_1_), custom_call_target="tpu_custom_call" | custom-call | flops 1000000 | bytes 1048576 | tf_op jit(solution)/shard_map/pallas_call | solution.py:248
  41.2 0.1 collective-permute-start.3
  41.3 0.1 collective-permute-start.4
  41.4 1.1 %collective-permute-done.5.refs_2_ = f32[4,64,128]{2,1,0:T(8,128)S(1)} collective-permute-done((f32[4,64,128]{2,1,0:T(8,128)S(1)}, f32[4,64,128]{2,1,0:T(8,128)S(1)}, u32[]{:S(2)}, u32[]{:S(2)}) %collective-permute-start.5) | collective-permute-done | bytes 131104 | tf_op jit(solution)/shard_map/ppermute | solution.py:300
  42.5 3.4 %shard_map.33.refs_2_ = f32[4,64,128]{2,1,0:T(8,128)S(1)} custom-call(s32[2944]{0:T(1024)S(1)} %pad_add_fusion.meta, bf16[8320,128]{1,0:T(8,128)(2,1)S(1)} %get-tuple-element.25.left, bf16[4096,256]{1,0:T(8,128)(2,1)S(1)} %get-tuple-element.30.refs_0_, f32[4,64,128]{2,1,0:T(8,128)S(1)} %get-tuple-element.33.refs_1_, ...), custom_call_target="tpu_custom_call" | custom-call | flops 1000000 | bytes 1048576 | tf_op jit(solution)/shard_map/pallas_call | solution.py:248
  45.8 3.4 %collective-permute-done.3.refs_0_ = f32[4,64,128]{2,1,0:T(8,128)S(1)} collective-permute-done((f32[4,64,128]{2,1,0:T(8,128)S(1)}, f32[4,64,128]{2,1,0:T(8,128)S(1)}, u32[]{:S(2)}, u32[]{:S(2)}) %collective-permute-start.3) | collective-permute-done | bytes 131104 | tf_op jit(solution)/shard_map/ppermute | solution.py:300
  49.2 0.8 %collective-permute-done.4.refs_1_ = f32[4,64,128]{2,1,0:T(8,128)S(1)} collective-permute-done((f32[4,64,128]{2,1,0:T(8,128)S(1)}, f32[4,64,128]{2,1,0:T(8,128)S(1)}, u32[]{:S(2)}, u32[]{:S(2)}) %collective-permute-start.4) | collective-permute-done | bytes 131104 | tf_op jit(solution)/shard_map/ppermute | solution.py:300
  50.0 0.9 %shard_map.34 = f32[256,128]{1,0:T(8,128)} custom-call(f32[4,64,128]{2,1,0:T(8,128)S(1)} %collective-permute-done.3.refs_0_, f32[4,64,128]{2,1,0:T(8,128)S(1)} %collective-permute-done.4.refs_1_, f32[4,64,128]{2,1,0:T(8,128)S(1)} %shard_map.33.refs_2_), custom_call_target="tpu_custom_call" | custom-call | tf_op jit(solution)/shard_map/pallas_call | solution.py:305
  (8 shorter events, 0.1 us)
Async XLA Ops:
  0.0 8.6 %collective-permute-start.1 = (f32[64,4096]{1,0:T(8,128)}, f32[64,4096]{1,0:T(8,128)S(1)}, u32[]{:S(2)}, u32[]{:S(2)}) collective-permute-start(f32[64,4096]{1,0:T(8,128)} %bitcast.29), channel_id=1, source_target_pairs={{0,1},{1,0},{2,3},{3,2},{4,5},{5,4},{6,7},{7,6},{8,9},{9,8},{10,11... | collective-permute-start | bytes 3145736 | tf_op jit(solution)/shard_map/ppermute | solution.py:274
  0.5 26.5 %collective-permute-start = (f32[64,4096]{1,0:T(8,128)}, f32[64,4096]{1,0:T(8,128)S(1)}, u32[]{:S(2)}, u32[]{:S(2)}) collective-permute-start(f32[64,4096]{1,0:T(8,128)} %bitcast.30), channel_id=1, source_target_pairs={{2,0},{3,1},{0,2},{1,3},{6,4},{7,5},{4,6},{5,7},{10,8},{11,9},{8,1... | collective-permute-start | bytes 3145736 | tf_op jit(solution)/shard_map/ppermute | solution.py:273
  8.6 1.2 %copy-start = (f32[1,64,4096]{2,1,0:T(8,128)S(1)}, f32[1,64,4096]{2,1,0:T(8,128)}, u32[]{:S(2)}) copy-start(f32[1,64,4096]{2,1,0:T(8,128)} %param.2) | copy-start | bytes 3145732
  27.0 3.0 %collective-permute-start.2 = (f32[64,4096]{1,0:T(8,128)S(1)}, f32[64,4096]{1,0:T(8,128)S(1)}, u32[]{:S(2)}, u32[]{:S(2)}) collective-permute-start(f32[64,4096]{1,0:T(8,128)S(1)} %collective-permute-done), channel_id=1, source_target_pairs={{0,1},{1,0},{2,3},{3,2},{4,5},{5,4},{6,7},{7,6},{8,9},{9,8},{10,11... | collective-permute-start | bytes 3145736 | tf_op jit(solution)/shard_map/ppermute | solution.py:285
  33.0 9.4 %collective-permute-start.5 = (f32[4,64,128]{2,1,0:T(8,128)S(1)}, f32[4,64,128]{2,1,0:T(8,128)S(1)}, u32[]{:S(2)}, u32[]{:S(2)}) collective-permute-start(f32[4,64,128]{2,1,0:T(8,128)S(1)} %get-tuple-element.34), channel_id=1, source_target_pairs={{0,8},{4,12},{8,0},{12,4},{1,9},{5,13},{9,1},{13,5},{2,10},{6,14},... | collective-permute-start | bytes 393224 | tf_op jit(solution)/shard_map/ppermute | solution.py:300
  41.2 8.0 %collective-permute-start.3 = (f32[4,64,128]{2,1,0:T(8,128)S(1)}, f32[4,64,128]{2,1,0:T(8,128)S(1)}, u32[]{:S(2)}, u32[]{:S(2)}) collective-permute-start(f32[4,64,128]{2,1,0:T(8,128)S(1)} %shard_map.31), channel_id=1, source_target_pairs={{0,12},{4,8},{8,4},{12,0},{1,13},{5,9},{9,5},{13,1},{2,14},{6,10},... | collective-permute-start | bytes 393224 | tf_op jit(solution)/shard_map/ppermute | solution.py:300
  41.3 8.7 %collective-permute-start.4 = (f32[4,64,128]{2,1,0:T(8,128)S(1)}, f32[4,64,128]{2,1,0:T(8,128)S(1)}, u32[]{:S(2)}, u32[]{:S(2)}) collective-permute-start(f32[4,64,128]{2,1,0:T(8,128)S(1)} %shard_map.32), channel_id=1, source_target_pairs={{0,4},{4,0},{8,12},{12,8},{1,5},{5,1},{9,13},{13,9},{2,6},{6,2},{1... | collective-permute-start | bytes 393224 | tf_op jit(solution)/shard_map/ppermute | solution.py:300

commit v4 on v3

--- a/solution.py
+++ b/solution.py
@@ -223,7 +223,9 @@
     return meta, (head, head + places)
 
 
-def products_of(columns, meta, layout, phase, places, left, rights, earlier, keep=False):
+def products_of(
+    columns, meta, layout, phase, places, left, rights, earlier, keep=False, work=1_000_000
+):
     smem = pl.BlockSpec(memory_space=pltpu.SMEM)
     vmem = pl.BlockSpec(memory_space=pltpu.VMEM)
     part = jax.ShapeDtypeStruct((SC // 2, BLK, LANES), jnp.float32)
@@ -256,7 +258,7 @@
         compiler_params=pltpu.CompilerParams(
             vmem_limit_bytes=16 * MIB + 8 * targets * LANES * LANES
         ),
-        cost_estimate=pl.CostEstimate(flops=1_000_000, bytes_accessed=MIB, transcendentals=0),
+        cost_estimate=pl.CostEstimate(flops=work, bytes_accessed=MIB, transcendentals=0),
     )(meta, *args)
 
 
@@ -271,10 +273,11 @@
     for hop in range(1, chips):
         jump = [((device + 2 * hop) % rows, device) for device in range(rows)]
         arriving.append(lax.ppermute(own_blocks, "row", jump))
-    sibling_blocks = lax.ppermute(own_blocks, "row", swap)
+    lists, own_again = lax.optimization_barrier((products[0, 0], own_blocks))
+    sibling_blocks = lax.ppermute(own_again, "row", swap)
 
     made = functools.partial(
-        products_of, columns, *plan(products[0, 0], slots, row, col, columns, chips)
+        products_of, columns, *plan(lists, slots, row, col, columns, chips)
     )
     whole = (0, columns)
     left, *parts = made(0, whole, own_blocks, [own_blocks, sibling_blocks], [])
@@ -284,9 +287,10 @@
     blocks, left, *parts = lax.optimization_barrier((arriving[-1], left, *parts))
     crossed = lax.ppermute(blocks, "row", swap)
 
-    arrived, early, begin = [], [], 0
+    arrived, early, begin, sums = [], [], 0, []
     for number, pairs in enumerate(sent_order(columns)):
         end = begin + len(pairs)
+        sums, parts = lax.optimization_barrier((sums, parts))
         places, earlier = (begin, end), parts[begin:end]
         if number == 0:
             right, *earlier = made(chips - 1, places, left, [blocks], earlier, keep=True)
@@ -294,7 +298,8 @@
         else:
             if pairs == [0]:
                 earlier = [*earlier, *early]
-            sums = made(chips - 1, places, left, [right], earlier)
+            work = 5_000_000_000 if pairs == [0] else 1_000_000
+            sums = made(chips - 1, places, left, [right], earlier, work=work)
         for pair, part in zip(pairs, sums):
             across = [(device, device ^ pair) for device in range(columns)]
             moved = lax.ppermute(part, "col", across) if pair else part

time: 50.5 us -> 48.1 us (0.952); the launches traced: 50.9 us -> 47.7 us
  Pallas kernels: 27.9 us -> 23.7 us
  starting transfers between devices: 4.93 us -> 6.02 us
    pallas_call x6, Pallas kernels: 26.9 us -> 22.8 us  [products_of(): pl.pallas_call(functools.partial(product_kernel, layout, bounds, new_left...]
    ppermute x3, waiting for transfers between devices: 5.29 us -> 4.24 us  [per_device(): moved = lax.ppermute(part, 'col', across) if pair else part]
    ppermute x3, starting transfers between devices: 1.99 us -> 3.01 us  [per_device(): moved = lax.ppermute(part, 'col', across) if pair else part]
    ppermute x1, waiting for transfers between devices: 5.87 us -> 6.65 us  [per_device(): arriving.append(lax.ppermute(own_blocks, 'row', jump))]
    unnamed x2 -> x3, local copies, waits for them, and re-layouts: 1.22 us -> 1.97 us
    slice x1, local copies, waits for them, and re-layouts: 0.73 us -> 0.02 us  [plan(): first, second, target = (lists[0], lists[1], lists[2])]
  transfers between devices with their start and end apart: 6 -> 6, of which waited for: 4 -> 2; matrix products, arithmetic and copies ran while one was open for 11% -> 12% of each run, Pallas kernels for 47% -> 42%
where the time goes in v4:
time: 48.1 us; the launch traced here: 47.7 us
  Pallas kernels  23.7 us (49%)
  waiting for transfers between devices  10.9 us (23%)
  starting transfers between devices  6.02 us (13%)
  other arithmetic  4.9 us (10%)
  local copies, waits for them, and re-layouts  1.99 us (4%)
    pallas_call x6, Pallas kernels, products_of(): pl.pallas_call(functools.partial(product_kernel, layout, bounds, new_left...  22.8 us
    ppermute x1, waiting for transfers between devices, per_device(): arriving.append(lax.ppermute(own_blocks, 'row', jump))  6.65 us
    sort x1, other arithmetic, plan(): codes, = lax.sort((segment << 13 | slot << 6 | second,), is_stable=False)  4.26 us
    ppermute x3, waiting for transfers between devices, per_device(): moved = lax.ppermute(part, 'col', across) if pair else part  4.24 us
    ppermute x3, starting transfers between devices, per_device(): moved = lax.ppermute(part, 'col', across) if pair else part  3.01 us
    ppermute x1, starting transfers between devices, per_device(): arriving.append(lax.ppermute(own_blocks, 'row', jump))  2.94 us
    unnamed x3, local copies, waits for them, and re-layouts  1.97 us
  transfers between devices with their start and end apart: 6, of which 2 were waited for; matrix products, arithmetic and copies ran while one was open for 12% of the time, Pallas kernels for 42%

profile of v4, /device:TPU:0, one launch (start us, length us, event | category | flops | bytes accessed | tf_op | source)
XLA Modules:
  0.0 47.7 jit_solution(1066332508978901482)
XLA Ops:
  0.0 2.9 %collective-permute-start = (f32[64,4096]{1,0:T(8,128)}, f32[64,4096]{1,0:T(8,128)S(1)}, u32[]{:S(2)}, u32[]{:S(2)}) collective-permute-start(f32[64,4096]{1,0:T(8,128)} %bitcast.32), channel_id=1, source_target_pairs={{2,0},{3,1},{0,2},{1,3},{6,4},{7,5},{4,6},{5,7},{10,8},{11,9},{8,1... | collective-permute-start | bytes 3145736 | tf_op jit(solution)/shard_map/ppermute | solution.py:275
  2.9 0.8 %copy.5 = s32[1,1,3,2048]{3,2,1,0:T(4,128)S(1)} copy(s32[1,1,3,2048]{3,1,2,0:T(1,128)} %param.3) | data formatting | bytes 49152
  3.7 0.1 collective-permute-start.1
  3.9 4.3 %sort.7 = s32[2048]{0:T(1024)S(1)} sort(s32[2048]{0:T(1024)S(1)} %fusion.8), dimensions={0}, to_apply=%region_0.1 | sort | flops 22528 | bytes 16384 | tf_op jit(solution)/shard_map/sort | solution.py:203
  8.1 0.2 select_reduce_fusion
  8.3 0.1 select_reduce_fusion.4
  8.5 0.1 select_reduce_fusion.5
  8.6 0.1 select_reduce_fusion.1
  8.8 0.0 collective-permute-done.1
  8.8 0.0 copy-start
  8.8 1.2 %copy-done = f32[1,64,4096]{2,1,0:T(8,128)S(1)} copy-done((f32[1,64,4096]{2,1,0:T(8,128)S(1)}, f32[1,64,4096]{2,1,0:T(8,128)}, u32[]{:S(2)}) %copy-start) | copy-done | bytes 1048600
  10.0 9.6 %shard_map.28 = (bf16[8320,128]{1,0:T(8,128)(2,1)S(1)}, f32[4,64,128]{2,1,0:T(8,128)S(1)}, f32[4,64,128]{2,1,0:T(8,128)S(1)}, f32[4,64,128]{2,1,0:T(8,128)S(1)}, f32[4,64,128]{2,1,0:T(8,128)S(1)}) custom-call(s32[2944]{0:T(1024)S(1)} %pad_add_fusion.meta, f32[2048,128]{1,0:T(8,128)S(1)} %bitcast.34, f32[2048,128]{1,0:T(8,128)S(1)} %bitcast.35, ...), custom_call_target="tpu_custom_call" | custom-call | flops 1000000 | bytes 1048576 | tf_op jit(solution)/shard_map/pallas_call | solution.py:250
  19.7 6.7 %collective-permute-done = f32[64,4096]{1,0:T(8,128)S(1)} collective-permute-done((f32[64,4096]{1,0:T(8,128)}, f32[64,4096]{1,0:T(8,128)S(1)}, u32[]{:S(2)}, u32[]{:S(2)}) %collective-permute-start) | collective-permute-done | bytes 1048608 | tf_op jit(solution)/shard_map/ppermute | solution.py:275
  26.3 0.0 collective-permute-start.2
  26.3 2.6 %shard_map.29 = (bf16[2048,256]{1,0:T(8,128)(2,1)S(1)}, f32[4,64,128]{2,1,0:T(8,128)S(1)}) custom-call(s32[2944]{0:T(1024)S(1)} %pad_add_fusion.meta, bf16[8320,128]{1,0:T(8,128)(2,1)S(1)} %get-tuple-element.39.left, f32[2048,128]{1,0:T(8,128)S(1)} %bitcast.37, f32[4,64,128]{2,1,0:T(8,128)S(1)} %get-tuple-element.45.refs_1_), custom_call_target="tpu_custom_call" | custom-call | flops 1000000 | bytes 1048576 | tf_op jit(solution)/shard_map/pallas_call | solution.py:250
  28.9 0.0 collective-permute-done.2
  29.0 2.7 %shard_map.30 = (bf16[4096,256]{1,0:T(8,128)(2,1)S(1)}, f32[4,64,128]{2,1,0:T(8,128)S(1)}) custom-call(s32[2944]{0:T(1024)S(1)} %pad_add_fusion.meta, bf16[8320,128]{1,0:T(8,128)(2,1)S(1)} %get-tuple-element.39.left, bf16[2048,256]{1,0:T(8,128)(2,1)S(1)} %get-tuple-element.46.refs_0_, f32[2048,128]{1,0:T(8,128)S(1)} %bitcast.36, ...), custom_call_target="tpu_custom_call" | custom-call | flops 1000000 | bytes 1048576 | tf_op jit(solution)/shard_map/pallas_call | solution.py:250
  31.6 2.5 %collective-permute-start.5 = (f32[4,64,128]{2,1,0:T(8,128)S(1)}, f32[4,64,128]{2,1,0:T(8,128)S(1)}, u32[]{:S(2)}, u32[]{:S(2)}) collective-permute-start(f32[4,64,128]{2,1,0:T(8,128)S(1)} %get-tuple-element.49), channel_id=1, source_target_pairs={{0,8},{4,12},{8,0},{12,4},{1,9},{5,13},{9,1},{13,5},{2,10},{6,14},... | collective-permute-start | bytes 393224 | tf_op jit(solution)/shard_map/ppermute | solution.py:305
  34.2 2.6 %shard_map.31 = f32[4,64,128]{2,1,0:T(8,128)S(1)} custom-call(s32[2944]{0:T(1024)S(1)} %pad_add_fusion.meta, bf16[8320,128]{1,0:T(8,128)(2,1)S(1)} %get-tuple-element.39.left, bf16[4096,256]{1,0:T(8,128)(2,1)S(1)} %get-tuple-element.48.refs_0_, f32[4,64,128]{2,1,0:T(8,128)S(1)} %get-tuple-element.53.refs_1_), custom_call_target="tpu_custom_call" | custom-call | flops 1000000 | bytes 1048576 | tf_op jit(solution)/shard_map/pallas_call | solution.py:250
  36.8 0.1 collective-permute-start.3
  36.9 2.6 %shard_map.32 = f32[4,64,128]{2,1,0:T(8,128)S(1)} custom-call(s32[2944]{0:T(1024)S(1)} %pad_add_fusion.meta, bf16[8320,128]{1,0:T(8,128)(2,1)S(1)} %get-tuple-element.39.left, bf16[4096,256]{1,0:T(8,128)(2,1)S(1)} %get-tuple-element.48.refs_0_, f32[4,64,128]{2,1,0:T(8,128)S(1)} %get-tuple-element.56.refs_1_), custom_call_target="tpu_custom_call" | custom-call | flops 1000000 | bytes 1048576 | tf_op jit(solution)/shard_map/pallas_call | solution.py:250
  39.5 0.4 collective-permute-start.4
  39.9 4.2 %collective-permute-done.5.refs_2_ = f32[4,64,128]{2,1,0:T(8,128)S(1)} collective-permute-done((f32[4,64,128]{2,1,0:T(8,128)S(1)}, f32[4,64,128]{2,1,0:T(8,128)S(1)}, u32[]{:S(2)}, u32[]{:S(2)}) %collective-permute-start.5) | collective-permute-done | bytes 131104 | tf_op jit(solution)/shard_map/ppermute | solution.py:305
  44.1 2.6 %shard_map.33.refs_2_ = f32[4,64,128]{2,1,0:T(8,128)S(1)} custom-call(s32[2944]{0:T(1024)S(1)} %pad_add_fusion.meta, bf16[8320,128]{1,0:T(8,128)(2,1)S(1)} %get-tuple-element.39.left, bf16[4096,256]{1,0:T(8,128)(2,1)S(1)} %get-tuple-element.48.refs_0_, f32[4,64,128]{2,1,0:T(8,128)S(1)} %get-tuple-element.58.refs_1_, ...), custom_call_target="tpu_custom_call" | custom-call | flops 5000000000 | bytes 1048576 | tf_op jit(solution)/shard_map/pallas_call | solution.py:250
  46.8 0.0 collective-permute-done.4.refs_1_
  46.8 0.0 collective-permute-done.3.refs_0_
  46.8 0.9 %shard_map.34 = f32[256,128]{1,0:T(8,128)} custom-call(f32[4,64,128]{2,1,0:T(8,128)S(1)} %collective-permute-done.3.refs_0_, f32[4,64,128]{2,1,0:T(8,128)S(1)} %collective-permute-done.4.refs_1_, f32[4,64,128]{2,1,0:T(8,128)S(1)} %shard_map.33.refs_2_), custom_call_target="tpu_custom_call" | custom-call | tf_op jit(solution)/shard_map/pallas_call | solution.py:310
  (9 shorter events, 0.1 us)
Async XLA Ops:
  0.0 26.3 %collective-permute-start = (f32[64,4096]{1,0:T(8,128)}, f32[64,4096]{1,0:T(8,128)S(1)}, u32[]{:S(2)}, u32[]{:S(2)}) collective-permute-start(f32[64,4096]{1,0:T(8,128)} %bitcast.32), channel_id=1, source_target_pairs={{2,0},{3,1},{0,2},{1,3},{6,4},{7,5},{4,6},{5,7},{10,8},{11,9},{8,1... | collective-permute-start | bytes 3145736 | tf_op jit(solution)/shard_map/ppermute | solution.py:275
  3.7 5.1 %collective-permute-start.1 = (f32[64,4096]{1,0:T(8,128)}, f32[64,4096]{1,0:T(8,128)S(1)}, u32[]{:S(2)}, u32[]{:S(2)}) collective-permute-start(f32[64,4096]{1,0:T(8,128)} %bitcast.33), channel_id=1, source_target_pairs={{0,1},{1,0},{2,3},{3,2},{4,5},{5,4},{6,7},{7,6},{8,9},{9,8},{10,11... | collective-permute-start | bytes 3145736 | tf_op jit(solution)/shard_map/ppermute | solution.py:277
  8.8 1.2 %copy-start = (f32[1,64,4096]{2,1,0:T(8,128)S(1)}, f32[1,64,4096]{2,1,0:T(8,128)}, u32[]{:S(2)}) copy-start(f32[1,64,4096]{2,1,0:T(8,128)} %param.2) | copy-start | bytes 3145732
  26.3 2.7 %collective-permute-start.2 = (f32[64,4096]{1,0:T(8,128)S(1)}, f32[64,4096]{1,0:T(8,128)S(1)}, u32[]{:S(2)}, u32[]{:S(2)}) collective-permute-start(f32[64,4096]{1,0:T(8,128)S(1)} %collective-permute-done), channel_id=1, source_target_pairs={{0,1},{1,0},{2,3},{3,2},{4,5},{5,4},{6,7},{7,6},{8,9},{9,8},{10,11... | collective-permute-start | bytes 3145736 | tf_op jit(solution)/shard_map/ppermute | solution.py:288
  31.6 12.5 %collective-permute-start.5 = (f32[4,64,128]{2,1,0:T(8,128)S(1)}, f32[4,64,128]{2,1,0:T(8,128)S(1)}, u32[]{:S(2)}, u32[]{:S(2)}) collective-permute-start(f32[4,64,128]{2,1,0:T(8,128)S(1)} %get-tuple-element.49), channel_id=1, source_target_pairs={{0,8},{4,12},{8,0},{12,4},{1,9},{5,13},{9,1},{13,5},{2,10},{6,14},... | collective-permute-start | bytes 393224 | tf_op jit(solution)/shard_map/ppermute | solution.py:305
  36.8 10.0 %collective-permute-start.3 = (f32[4,64,128]{2,1,0:T(8,128)S(1)}, f32[4,64,128]{2,1,0:T(8,128)S(1)}, u32[]{:S(2)}, u32[]{:S(2)}) collective-permute-start(f32[4,64,128]{2,1,0:T(8,128)S(1)} %shard_map.31), channel_id=1, source_target_pairs={{0,12},{4,8},{8,4},{12,0},{1,13},{5,9},{9,5},{13,1},{2,14},{6,10},... | collective-permute-start | bytes 393224 | tf_op jit(solution)/shard_map/ppermute | solution.py:305
  39.5 7.3 %collective-permute-start.4 = (f32[4,64,128]{2,1,0:T(8,128)S(1)}, f32[4,64,128]{2,1,0:T(8,128)S(1)}, u32[]{:S(2)}, u32[]{:S(2)}) collective-permute-start(f32[4,64,128]{2,1,0:T(8,128)S(1)} %shard_map.32), channel_id=1, source_target_pairs={{0,4},{4,0},{8,12},{12,8},{1,5},{5,1},{9,13},{13,9},{2,6},{6,2},{1... | collective-permute-start | bytes 393224 | tf_op jit(solution)/shard_map/ppermute | solution.py:305
